TPU v7x, 32 devices: a whole 2x2x4 slice. The times are simulated.
32 devices in a mesh: gop: 4 (over z), row: 8 (over y, x, core).
Axes of the slice: x: 2, y: 2, z: 4, core: 2. Of those that a mesh axis runs over, the one named last changes fastest.
Arguments:
- features: bfloat16 [4, 256, 480, 128], P('gop', 'row'), may hold values from -6 to 6
- filters: bfloat16 [3, 256, 2, 480, 128], P(None, None, None, 'row'), may hold values from -2.390625 to 2.390625
- anchors: int32 [4, 2], replicated, may hold values from 0 to 3, as said below
Outputs:
- joined: bfloat16 [4, 256, 480, 128], P('gop', 'row')
Inputs may be any that keep to these rules, and one draw needn't show every extreme that they name: anchors[:, 0] lists each of the 4 frames exactly once; anchors[:, 1] takes exactly two distinct values, each in half of the rows.
All inputs are finite; a program needn't handle non-finite values.
Results may differ from a plain program's by a relative error of at most 0.0062.
Values may be sent and summed in bfloat16 or wider, within the bound.
A program may use at most 256 MiB of HBM per device.

v0:
```python
import math

import jax
import jax.numpy as jnp
from jax import lax
from jax.sharding import PartitionSpec as P


def row_table(length):
    across = jnp.arange(length, dtype=jnp.int32)
    phases = across[:, None] * across[None, :] % length
    angles = phases.astype(jnp.float32) * (2.0 * math.pi / length)
    factor = 1.0 / math.sqrt(length)
    return jnp.concatenate([jnp.cos(angles) * factor, -jnp.sin(angles) * factor], axis=1).astype(
        jnp.bfloat16
    )


def column_matrix(length, sign):
    across = jnp.arange(length, dtype=jnp.int32)
    phases = across[:, None] * across[None, :] % length
    angles = phases.astype(jnp.float32) * (2.0 * math.pi / length)
    factor = 1.0 / math.sqrt(length)
    cosine = jnp.cos(angles) * factor
    sine_part = sign * jnp.sin(angles) * factor
    upper = jnp.stack([cosine, -sine_part], axis=-1)
    lower = jnp.stack([sine_part, cosine], axis=-1)
    return jnp.stack([upper, lower], axis=1).reshape(2 * length, 2 * length).astype(jnp.bfloat16)


def on_device(features, filters, anchors):
    frames_here = features.shape[0]
    columns = features.shape[2]
    height = filters.shape[1]
    forward_rows = row_table(columns)
    split_table = forward_rows.reshape(columns, 2, columns)
    forward_cols = column_matrix(height, -1.0)
    inverse_cols = column_matrix(height, 1.0)
    first_frame = lax.axis_index("gop") * frames_here
    own_anchors = lax.dynamic_slice_in_dim(anchors, first_frame, frames_here, 0)
    count = features.shape[0]
    done = jnp.einsum("nhwc,wk->nhkc", features, forward_rows, preferred_element_type=jnp.float32)
    slab = lax.all_to_all(
        done.astype(jnp.bfloat16).reshape(count, features.shape[1], 2, columns, features.shape[3]),
        "row",
        split_axis=3,
        concat_axis=1,
        tiled=True,
    )
    shape_in = slab.shape
    merged = slab.reshape(shape_in[0], 2 * shape_in[1], shape_in[3] * shape_in[4])

    def one_frame(matrix):
        return jnp.dot(forward_cols, matrix, preferred_element_type=jnp.float32).astype(
            jnp.bfloat16
        )

    own_spec = lax.map(one_frame, merged).reshape(shape_in)
    empty = jnp.zeros_like(own_spec)
    totals = (empty, empty)
    shards = lax.all_gather(own_spec, "gop", axis=0, tiled=True)
    amount = shards.shape[0]
    results = []
    for anchor_slot in range(2):
        wanted = own_anchors[:, anchor_slot]
        inside = jnp.logical_and(wanted >= 0, wanted < amount)
        position = jnp.clip(wanted, 0, amount - 1)
        picked = jnp.take(shards, position, axis=0)
        inside = inside.reshape((-1,) + (1,) * (shards.ndim - 1))
        results.append(jnp.where(inside, picked, totals[anchor_slot]))
    first_spec = results[0]
    second_spec = results[1]
    sources = (own_spec, first_spec, second_spec)
    real_part = jnp.zeros(own_spec[:, :, 0].shape, jnp.float32)
    imag_part = jnp.zeros(own_spec[:, :, 0].shape, jnp.float32)
    for which_one in range(3):
        source_real = sources[which_one][:, :, 0].astype(jnp.float32)
        source_imag = sources[which_one][:, :, 1].astype(jnp.float32)
        gain_real = filters[which_one, :, 0].astype(jnp.float32)
        gain_imag = filters[which_one, :, 1].astype(jnp.float32)
        real_part = real_part + gain_real * source_real - gain_imag * source_imag
        imag_part = imag_part + gain_real * source_imag + gain_imag * source_real
    mixed = jnp.stack([real_part, imag_part], axis=2).astype(jnp.bfloat16)
    mixed_shape = mixed.shape
    merged = mixed.reshape(mixed_shape[0], 2 * mixed_shape[1], mixed_shape[3] * mixed_shape[4])

    def invert_frame(matrix):
        return jnp.dot(inverse_cols, matrix, preferred_element_type=jnp.float32).astype(
            jnp.bfloat16
        )

    back = lax.map(invert_frame, merged).reshape(mixed_shape)
    spatial = jnp.einsum(
        "nhpkc,wpk->nhwc",
        lax.all_to_all(back, "row", split_axis=1, concat_axis=3, tiled=True),
        split_table,
        preferred_element_type=jnp.float32,
    )
    return (features.astype(jnp.float32) + spatial).astype(jnp.bfloat16)


def solution(mesh):
    in_specs = (P("gop", "row", None, None), P(None, None, None, "row", None), P())
    out_specs = P("gop", "row", None, None)
    return jax.shard_map(
        on_device, mesh=mesh, in_specs=in_specs, out_specs=out_specs, check_vma=False
    )
```

profile of v0, /device:TPU:31, one launch (start us, length us, event | category | flops | bytes accessed | tf_op | source)
XLA Modules:
  0.0 937.9 jit_solution(5133501088576465107)
XLA Ops:
  10.8 7.3 convolution_convert_fusion.2
  18.1 8.2 copy.39
  26.3 5.6 all-to-all-start
  37.7 26.2 %copy.38 = bf16[256,2,256,2]{3,2,1,0:T(8,128)(2,1)} copy(bf16[256,2,256,2]{2,0,3,1:T(8,128)(2,1)S(1)} %get-tuple-element.58) | data formatting | bytes 1048576 | tf_op jit(solution)/shard_map/stack | solution.py:28
  63.9 48.9 %convert_element_type.217 = bf16[512,512]{1,0:T(8,128)(2,1)S(1)} reshape(bf16[256,2,256,2]{3,2,1,0:T(8,128)(2,1)} %copy.38) | data formatting | bytes 1048576 | tf_op jit(solution)/shard_map/convert_element_type | solution.py:28
  117.7 7.7 copy.40
  125.5 9.6 %copy.41 = bf16[1,8,32,2,60,128]{5,4,3,2,1,0:T(8,128)(2,1)} copy(bf16[1,8,32,2,60,128]{5,2,4,1,3,0:T(8,128)(2,1)} %bitcast.61) | data formatting | bytes 15728640 | tf_op jit(solution)/shard_map/all_to_all | solution.py:43
  135.0 16.1 %convolution_convert_fusion.1 = bf16[512,7680]{1,0:T(8,128)(2,1)} fusion(bf16[512,512]{1,0:T(8,128)(2,1)S(1)} %convert_element_type.217, bf16[64,8,60,128]{3,2,1,0:T(8,128)(2,1)} %bitcast.64), kind=kOutput, calls=%fused_computation.1 | convolution fusion | flops 4030464000 | bytes 16252928 | tf_op jit(solution)/shard_map/while/body/eval_jaxpr/dot_general | solution.py:54
  151.2 12.6 %reshape.320 = bf16[1,256,2,60,128]{4,3,2,1,0:T(8,128)(2,1)} reshape(bf16[512,7680]{1,0:T(8,128)(2,1)} %convolution_convert_fusion.1) | data formatting | bytes 15728640 | tf_op jit(solution)/shard_map/reshape | solution.py:58
  163.8 11.6 %copy.44 = bf16[1,256,2,60,128]{4,1,3,2,0:T(8,128)(2,1)} copy(bf16[1,256,2,60,128]{4,3,2,1,0:T(8,128)(2,1)} %reshape.320) | data formatting | bytes 15728640 | tf_op jit(solution)/shard_map/reshape | solution.py:58
  180.2 23.1 %copy.36 = bf16[256,2,256,2]{3,2,1,0:T(8,128)(2,1)} copy(bf16[256,2,256,2]{2,0,3,1:T(8,128)(2,1)S(1)} %get-tuple-element.57) | data formatting | bytes 1048576 | tf_op jit(solution)/shard_map/stack | solution.py:28
  203.3 49.0 %convert_element_type.215 = bf16[512,512]{1,0:T(8,128)(2,1)S(1)} reshape(bf16[256,2,256,2]{3,2,1,0:T(8,128)(2,1)} %copy.36) | data formatting | bytes 1048576 | tf_op jit(solution)/shard_map/convert_element_type | solution.py:28
  252.3 47.5 %fusion.51 = (bf16[1,256,1,60,128]{4,2,3,1,0:T(2,128)(2,1)}, bf16[1,256,1,60,128]{4,2,3,1,0:T(2,128)(2,1)}, bf16[1,256,1,60,128]{4,2,3,1,0:T(2,128)(2,1)}, bf16[...) fusion(bf16[3,256,2,60,128]{4,2,3,1,0:T(2,128)(2,1)} %param.6), kind=kLoop, calls=%fused_computation.95 | loop fusion | bytes 47185920 | tf_op jit(solution)/shard_map/slice | solution.py:79
  299.8 401.3 %all-gather.2.cloned.1.call-done = bf16[4,256,2,60,128]{4,1,3,2,0:T(8,128)(2,1)} async-done(((bf16[1,256,2,60,128]{4,1,3,2,0:T(8,128)(2,1)}), bf16[4,256,2,60,128]{4,1,3,2,0:T(8,128)(2,1)}) %all-gather.2.cloned.1.call-update) | async-done | bytes 31457296 | tf_op jit(solution)/shard_map/all_gather | solution.py:61
  701.1 11.6 %constant_dynamic-slice_fusion.1 = (bf16[1,256,2,60,128]{4,1,3,2,0:T(8,128)(2,1)}, bf16[1,256,2,60,128]{4,1,3,2,0:T(8,128)(2,1)}) fusion(bf16[4,256,2,60,128]{4,1,3,2,0:T(8,128)(2,1)} %all-gather.2.cloned.1.call-done, s32[]{:T(128)} %bitcast.15, s32[]{:T(128)} %bitcast.19), kind=kLoop, calls=%fused_computation.91 | loop fusion | bytes 31457288 | tf_op jit(solution)/shard_map/jit(_take)/gather | solution.py:68
  712.7 13.7 %fusion.12 = bf16[1,256,2,60,128]{4,3,2,1,0:T(8,128)(2,1)} fusion(bf16[1,256,2,60,128]{4,1,3,2,0:T(8,128)(2,1)} %get-tuple-element.44, pred[]{:T(512)} %bitcast.18, pred[]{:T(512)} %bitcast.16), kind=kLoop, calls=%fused_computation.28 | loop fusion | flops 7864320 | bytes 15728642 | tf_op jit(solution)/shard_map/jit(_where)/select_n | solution.py:70
  726.4 13.9 %fusion.13 = bf16[1,256,2,60,128]{4,3,2,1,0:T(8,128)(2,1)} fusion(bf16[1,256,2,60,128]{4,1,3,2,0:T(8,128)(2,1)} %get-tuple-element.43, pred[]{:T(512)} %bitcast.14, pred[]{:T(512)} %bitcast.12), kind=kLoop, calls=%fused_computation.30 | loop fusion | flops 7864320 | bytes 15728642 | tf_op jit(solution)/shard_map/jit(_where)/select_n | solution.py:70
  740.2 27.4 %fusion.5 = (bf16[1,256,1,60,128]{4,3,2,1,0:T(8,128)(2,1)S(1)}, bf16[1,256,1,60,128]{4,3,2,1,0:T(8,128)(2,1)}) fusion(bf16[1,256,2,60,128]{4,3,2,1,0:T(8,128)(2,1)} %fusion.12, bf16[1,256,2,60,128]{4,3,2,1,0:T(8,128)(2,1)} %fusion.13, bf16[1,256,2,60,128]{4,3,2,1,0:T(8,128)(2,1)} %reshape.320, bf16[1,256,1,60,128]{4,2,3,1,0:T(2,128)(2,1)} %get-tuple-element.50, ...), kind=kLoop, calls=%fused_computation.19 | loop fusion | flops 70778880 | bytes 55050240 | tf_op jit(solution)/shard_map/convert
  767.7 6.3 pad_maximum_fusion
  774.0 16.3 %convolution_convert_fusion = bf16[512,7680]{1,0:T(8,128)(2,1)} fusion(bf16[512,512]{1,0:T(8,128)(2,1)S(1)} %convert_element_type.215, bf16[64,8,60,128]{3,2,1,0:T(8,128)(2,1)} %bitcast.63), kind=kOutput, calls=%fused_computation | convolution fusion | flops 4030464000 | bytes 16252928 | tf_op jit(solution)/shard_map/while/body/eval_jaxpr/dot_general | solution.py:88
  790.3 12.4 %reshape.321 = bf16[1,256,2,60,128]{4,3,2,1,0:T(8,128)(2,1)} reshape(bf16[512,7680]{1,0:T(8,128)(2,1)} %convolution_convert_fusion) | data formatting | bytes 15728640 | tf_op jit(solution)/shard_map/reshape | solution.py:92
  802.7 15.4 %copy.50 = bf16[1,256,2,60,128]{4,2,3,0,1:T(2,128)(2,1)} copy(bf16[1,256,2,60,128]{4,3,2,1,0:T(8,128)(2,1)} %reshape.321) | data formatting | bytes 15728640 | tf_op jit(solution)/shard_map/reshape | solution.py:92
  827.9 81.5 %all-to-all-done.1 = bf16[1,256,2,60,128]{4,2,3,0,1:T(2,128)(2,1)} async-done(((bf16[1,256,2,60,128]{4,2,3,0,1:T(2,128)(2,1)}), bf16[1,256,2,60,128]{4,2,3,0,1:T(2,128)(2,1)}, u32[]{:S(2)}, u32[]{:S(2)}) %all-to-all-start.1) | async-done | bytes 7864352 | tf_op jit(solution)/shard_map/all_to_all | solution.py:95
  919.7 11.1 %fusion.18 = bf16[1,32,480,128]{3,2,1,0:T(8,128)(2,1)} fusion(bf16[1,32,480,128]{3,2,1,0:T(8,128)(2,1)} %param.5, bf16[32,2,480,128]{3,0,2,1:T(8,128)(2,1)} %bitcast.65, bf16[480,1,480]{2,0,1:T(8,128)(2,1)S(1)} %get-tuple-element.61, bf16[480,1,480]{2,0,1:T(8,128)(2,1)S(1)} %get-tuple-element.62), kind=kOutput, calls=%fused_computation.36 | convolution fusion | flops 3782615040 | bytes 16650240 | tf_op jit(solution)/shard_map/nhpkc,wpk->nhwc/dot_general | solution.py:93
  (21 shorter events, 35.7 us)
Async XLA Ops:
  6.5 168.9 %copy-start = (s32[4,2]{0,1:T(2,128)S(1)}, s32[4,2]{0,1:T(2,128)}, u32[]{:S(2)}) copy-start(s32[4,2]{0,1:T(2,128)} %param.7) | copy-start | bytes 100
  26.3 91.4 %all-to-all-start = ((bf16[1,32,2,480,128]{4,1,2,0,3:T(8,128)(2,1)}), bf16[1,32,2,480,128]{4,1,2,0,3:T(8,128)(2,1)}, u32[]{:S(2)}, u32[]{:S(2)}) async-start(bf16[1,32,2,480,128]{4,1,2,0,3:T(8,128)(2,1)} %copy.39), calls=%async_computation | async-start | bytes 15728640 | tf_op jit(solution)/shard_map/all_to_all | solution.py:43
  31.9 669.2 %all-gather.2.cloned.1.call-start = ((), (), s32[]{:S(2)}) async-start(), calls=%async_computation.2 | async-start | bytes 39321600 | tf_op jit(solution)/shard_map/all_gather | solution.py:61
  818.1 91.3 %all-to-all-start.1 = ((bf16[1,256,2,60,128]{4,2,3,0,1:T(2,128)(2,1)}), bf16[1,256,2,60,128]{4,2,3,0,1:T(2,128)(2,1)}, u32[]{:S(2)}, u32[]{:S(2)}) async-start(bf16[1,256,2,60,128]{4,2,3,0,1:T(2,128)(2,1)} %copy.50), calls=%async_computation.1 | async-start | bytes 15728640 | tf_op jit(solution)/shard_map/all_to_all | solution.py:95
  919.7 11.1 %copy-start.1 = (s32[4,2]{0,1:T(2,128)S(1)}, s32[4,2]{0,1:T(2,128)}, u32[]{:S(2)}) copy-start(s32[4,2]{0,1:T(2,128)} %param.7) | copy-start | bytes 100
Sparse Core Ops, SparseCore 0:
  175.6 525.4 all-gather.1
where the time goes:
time: 952 us; the launch traced here: 938 us
  waiting for transfers between devices  488 us (51%)
  local copies, waits for them, and re-layouts  295 us (31%)
  other arithmetic  75 us (8%)
  matrix products  50.8 us (5%)
  between operations  17.8 us (2%)
  starting transfers between devices  11.7 us (1%)
    all_gather x1, waiting for transfers between devices, on_device(): shards = lax.all_gather(own_spec, 'gop', axis=0, tiled=True)  401 us
    convert_element_type x2, local copies, waits for them, and re-layouts, column_matrix(): jnp.stack([upper, lower], axis=1).reshape(2 * length, 2 * length)  97.9 us
    all_to_all x1, waiting for transfers between devices, on_device(): lax.all_to_all(back, 'row', split_axis=1, concat_axis=3, tiled=True)  81.5 us
    another operation x2, local copies, waits for them, and re-layouts, column_matrix(): jnp.stack([upper, lower], axis=1).reshape(2 * length, 2 * length)  49.3 us
    slice x1, local copies, waits for them, and re-layouts, on_device(): gain_real = filters[which_one, :, 0].astype(jnp.float32)  47.5 us
    another operation x8, other arithmetic  40.9 us
    reshape x2, local copies, waits for them, and re-layouts, on_device(): back = lax.map(invert_frame, merged).reshape(mixed_shape)  27.8 us
    select_n x2, other arithmetic, on_device(): results.append(jnp.where(inside, picked, totals[anchor_slot]))  27.6 us
  transfers between devices with their start and end apart: 3, of which 3 were waited for; matrix products, arithmetic and copies ran while one was open for 22% of the time, Pallas kernels for 0%

commit v1 on v0

v1 whole, which is shorter than its diff:
```python
import functools
import math

import jax
import jax.numpy as jnp
import ml_dtypes
import numpy as np
from jax import lax
from jax.experimental import pallas as pl
from jax.experimental.pallas import tpu as pltpu
from jax.sharding import PartitionSpec as P

WINDOW = 8
VMEM_LIMIT = 56 * 1024 * 1024


def trig(length, first, second):
    phases = (first[:, None].astype(np.int64) * second[None, :]) % length
    angles = phases.astype(np.float32) * np.float32(2.0 * math.pi / length)
    factor = np.float32(1.0 / math.sqrt(length))
    return np.cos(angles) * factor, np.sin(angles) * factor


def layout(gops, rows, width):
    per_row = width // rows
    each = -(-(per_row + 1) // (2 * gops))
    columns = []
    for g in range(gops):
        for r in range(rows):
            second = r >= rows // 2
            pair = rows - 1 - r if second else r
            for i in range(each):
                s = 2 * each * g + (each if second else 0) + i
                columns.append(per_row * pair + s if s <= per_row else -1)
    return each, np.array(columns)


def row_rows(gops, rows, width):
    each, columns = layout(gops, rows, width)
    cosine, sine = trig(width, np.maximum(columns, 0), np.arange(width))
    table = np.stack([cosine, -sine], axis=1) * (columns >= 0)[:, None, None]
    return table.reshape(2 * len(columns), width).astype(ml_dtypes.bfloat16)


def column_matrix(length, sign):
    across = np.arange(length)
    cosine, sine = trig(length, across, across)
    sine = np.float32(sign) * sine
    return np.block([[cosine, -sine], [sine, cosine]]).astype(ml_dtypes.bfloat16)


def forward_kernel(rows_each, table_ref, x_ref, o_ref, turned):
    for h in range(0, rows_each, 2):
        pair = jnp.concatenate([x_ref[h], x_ref[h + 1]], axis=1)
        done = jnp.dot(table_ref[...], pair, preferred_element_type=jnp.float32)
        count = done.shape[0]
        turned[pl.ds(h, count, stride=rows_each), :] = done[:, :128]
        turned[pl.ds(h + 1, count, stride=rows_each), :] = done[:, 128:]
    o_ref[...] = turned[...].astype(jnp.bfloat16).reshape(o_ref.shape)


def forward_rows(table, x):
    h, w, c = x.shape
    count = table.shape[0]
    block = 16
    return pl.pallas_call(
        functools.partial(forward_kernel, block),
        grid=(h // block,),
        in_specs=[
            pl.BlockSpec((count, w), lambda i: (0, 0)),
            pl.BlockSpec((block, w, c), lambda i: (i, 0, 0)),
        ],
        out_specs=pl.BlockSpec((count, block, c), lambda i: (0, i, 0)),
        out_shape=jax.ShapeDtypeStruct((count, h, c), jnp.bfloat16),
        scratch_shapes=[pltpu.VMEM((count * block, c), jnp.float32)],
        compiler_params=pltpu.CompilerParams(vmem_limit_bytes=VMEM_LIMIT),
    )(table, x)


def inverse_kernel(rows_each, table_ref, b_ref, x_ref, o_ref, turned):
    turned[...] = b_ref[...].reshape(turned.shape).astype(jnp.float32)
    count = table_ref.shape[1]
    for h in range(0, rows_each, 2):
        pair = jnp.concatenate(
            [turned[pl.ds(h + d, count, stride=rows_each), :] for d in range(2)], axis=1
        ).astype(jnp.bfloat16)
        done = jnp.dot(table_ref[...], pair, preferred_element_type=jnp.float32)
        for d in range(2):
            added = x_ref[h + d].astype(jnp.float32) + done[:, 128 * d : 128 * d + 128]
            o_ref[h + d] = added.astype(jnp.bfloat16)


def inverse_rows(table, back, x):
    h, w, c = x.shape
    count = table.shape[1]
    block = 16
    return pl.pallas_call(
        functools.partial(inverse_kernel, block),
        grid=(h // block,),
        in_specs=[
            pl.BlockSpec((w, count), lambda i: (0, 0)),
            pl.BlockSpec((count, block, c), lambda i: (0, i, 0)),
            pl.BlockSpec((block, w, c), lambda i: (i, 0, 0)),
        ],
        out_specs=pl.BlockSpec((block, w, c), lambda i: (i, 0, 0)),
        out_shape=jax.ShapeDtypeStruct((h, w, c), jnp.bfloat16),
        scratch_shapes=[pltpu.VMEM((count * block, c), jnp.float32)],
        compiler_params=pltpu.CompilerParams(vmem_limit_bytes=VMEM_LIMIT),
    )(table, back, x)


def middle_kernel(
    frames, rows, height,
    place_ref, weight_ref, anchor_ref, x_ref, p_ref, n_ref, mf_ref, mi_ref, o_ref,
    p_wide, n_wide, spec, mixed,
):
    slot = pl.program_id(0)
    lines = 2 * WINDOW

    @pl.when(slot == 0)
    def _():
        def widen(k, carry):
            mirror = lax.rem(height - k, height)
            for j in range(3):
                at = pl.ds(pl.multiple_of((j * height + k) * lines, lines), lines)
                p_wide[at, :] = p_ref[j, k].astype(jnp.float32)
                n_wide[at, :] = n_ref[j, mirror].astype(jnp.float32)
            return carry

        lax.fori_loop(0, height, widen, 0, unroll=4)

    short = x_ref.shape[2]
    for f in range(0, frames, 2):
        sides = []
        for d in range(2):
            sides.append(
                jnp.concatenate(
                    [x_ref[(f + d) * rows + r, q] for q in range(2) for r in range(rows)], axis=0
                )
            )
        done = jnp.dot(
            mf_ref[...], jnp.concatenate(sides, axis=1), preferred_element_type=jnp.float32
        ).astype(jnp.bfloat16)
        spec[f] = done[:, :128]
        spec[f + 1] = done[:, 128:]

    place_p, place_n = place_ref[0, slot], place_ref[1, slot]
    weight_p, weight_n = weight_ref[0, slot], weight_ref[1, slot]
    chunk = 32

    def mix(step, carry):
        k = pl.multiple_of(step * chunk, chunk)
        gains = []
        for j in range(3):
            parts = []
            for p in range(2):
                start = (j * height + k) * lines + p * WINDOW
                right = p_wide[pl.ds(start + place_p, chunk, stride=lines), :]
                left = n_wide[pl.ds(start + place_n, chunk, stride=lines), :]
                left = left * weight_n
                parts.append(right * weight_p + (left if p == 0 else -left))
            gains.append(parts)
        for f in range(frames):
            real, imag = None, None
            for j in range(3):
                source = f if j == 0 else anchor_ref[f, j - 1]
                s_real = spec[source, pl.ds(k, chunk), :].astype(jnp.float32)
                s_imag = spec[source, pl.ds(height + k, chunk), :].astype(jnp.float32)
                g_real, g_imag = gains[j]
                new_real = g_real * s_real - g_imag * s_imag
                new_imag = g_real * s_imag + g_imag * s_real
                real = new_real if real is None else real + new_real
                imag = new_imag if imag is None else imag + new_imag
            lanes = pl.ds(f * 128, 128)
            mixed[pl.ds(k, chunk), lanes] = real.astype(jnp.bfloat16)
            mixed[pl.ds(height + k, chunk), lanes] = imag.astype(jnp.bfloat16)
        return carry

    lax.fori_loop(0, height // chunk, mix, 0)

    for f in range(0, frames, 2):
        back = jnp.dot(
            mi_ref[...], mixed[:, 128 * f : 128 * f + 256], preferred_element_type=jnp.float32
        ).astype(jnp.bfloat16)
        for d in range(2):
            for q in range(2):
                for r in range(rows):
                    at = q * height + r * short
                    o_ref[(f + d) * rows + r, q] = back[at : at + short, 128 * d : 128 * d + 128]


def middle(frames, rows, place, weight, anchors, x, plus, minus, mf, mi):
    n, count, short, c = x.shape
    height = plus.shape[1]
    whole = lambda shape: pl.BlockSpec(shape, lambda i: (0,) * len(shape))
    smem = pl.BlockSpec(memory_space=pltpu.SMEM)
    block = pl.BlockSpec((n, 2, short, c), lambda i: (0, i, 0, 0))
    return pl.pallas_call(
        functools.partial(middle_kernel, frames, rows, height),
        grid=(count // 2,),
        in_specs=[smem, smem, smem, block, whole(plus.shape), whole(minus.shape),
                  whole(mf.shape), whole(mi.shape)],
        out_specs=block,
        out_shape=jax.ShapeDtypeStruct(x.shape, jnp.bfloat16),
        scratch_shapes=[
            pltpu.VMEM((3 * height * 2 * WINDOW, c), jnp.float32),
            pltpu.VMEM((3 * height * 2 * WINDOW, c), jnp.float32),
            pltpu.VMEM((frames, 2 * height, c), jnp.bfloat16),
            pltpu.VMEM((2 * height, frames * c), jnp.bfloat16),
        ],
        compiler_params=pltpu.CompilerParams(vmem_limit_bytes=VMEM_LIMIT),
    )(place, weight, anchors, x, plus, minus, mf, mi)


def on_device(gops, rows, features, filters, anchors):
    h, w, c = features.shape[1:]
    height = filters.shape[1]
    per_row = filters.shape[3]
    devices = gops * rows
    table = row_rows(gops, rows, w)
    each, _ = layout(gops, rows, w)
    g, r = lax.axis_index("gop"), lax.axis_index("row")
    second = r >= rows // 2

    slots = 2 * each * g + jnp.where(second, each, 0) + jnp.arange(each)
    theirs = 2 * each * g + jnp.where(second, 0, each) + jnp.arange(each)
    limit = per_row - WINDOW
    start_plus = lambda s: jnp.clip(s[0], 0, limit)
    start_minus = lambda s: jnp.clip(per_row - s[each - 1], 0, limit)
    cut = lambda start: lax.dynamic_slice_in_dim(filters, start, WINDOW, 3).reshape(
        3, height, 2 * WINDOW, c
    )
    to_send = cut(jnp.where(second, start_minus(theirs), start_plus(theirs)))
    got = lax.ppermute(to_send, "row", [(i, rows - 1 - i) for i in range(rows)])
    own = cut(jnp.where(second, start_minus(slots), start_plus(slots)))
    plus = jnp.where(second, got, own)
    minus = jnp.where(second, own, got)
    place = jnp.stack([slots - start_plus(slots), per_row - slots - start_minus(slots)])
    place = jnp.clip(place, 0, WINDOW - 1).astype(jnp.int32)
    weight = jnp.stack([slots < per_row, (slots >= 1) & (slots <= per_row)]).astype(jnp.float32)

    done = forward_rows(jnp.asarray(table), features[0])
    slab = lax.all_to_all(
        done.reshape(devices, 2 * each, h, c), ("gop", "row"), split_axis=0, concat_axis=0, tiled=True
    )
    back = middle(
        gops, rows, place, weight, anchors, slab, plus, minus,
        jnp.asarray(column_matrix(height, -1.0)), jnp.asarray(column_matrix(height, 1.0)),
    )
    back = lax.all_to_all(back, ("gop", "row"), split_axis=0, concat_axis=0, tiled=True)
    joined = inverse_rows(jnp.asarray(table.T), back.reshape(devices * 2 * each, h, c), features[0])
    return joined[None]


def solution(mesh):
    in_specs = (P("gop", "row", None, None), P(None, None, None, "row", None), P())
    out_specs = P("gop", "row", None, None)
    return jax.shard_map(
        functools.partial(on_device, mesh.shape["gop"], mesh.shape["row"]),
        mesh=mesh, in_specs=in_specs, out_specs=out_specs, check_vma=False,
    )
```

time: 952 us -> 270 us (0.28); the launches traced: 938 us -> 266 us
  waiting for transfers between devices: 488 us -> 105 us
  local copies, waits for them, and re-layouts: 295 us -> 11.3 us
  blocking collectives: 0 us -> 99.3 us
  other arithmetic: 75 us -> 6.34 us
  matrix products: 50.8 us -> 0 us
  Pallas kernels: 0 us -> 34.6 us
  between operations: 17.8 us -> 2.64 us
    all_gather x1 -> x0, waiting for transfers between devices: 401 us -> none  [on_device(): shards = lax.all_gather(own_spec, 'gop', axis=0, tiled=True)]
    ppermute x0 -> x1, waiting for transfers between devices: none -> 105 us  [on_device(): got = lax.ppermute(to_send, 'row', [(i, rows - 1 - i) for i in range(rows)])]
    all_to_all x0 -> x1, blocking collectives: none -> 99.3 us  [on_device(): lax.all_to_all(back, ('gop', 'row'), split_axis=0, concat_axis=0, tiled=T...]
    convert_element_type x2 -> x0, local copies, waits for them, and re-layouts: 97.9 us -> none  [column_matrix(): jnp.stack([upper, lower], axis=1).reshape(2 * length, 2 * length)]
    all_to_all x2 -> x1, waiting for transfers between devices: 86.4 us -> 0.01 us  [on_device(): lax.all_to_all(done.reshape(devices, 2 * each, h, c), ('gop', 'row'), spl...]
    reshape x5 -> x0, local copies, waits for them, and re-layouts: 60.3 us -> none  [the longest x2 27.8 us: on_device(): back = lax.map(invert_frame, merged).reshape(mixed_shape)]
    dot_general x4 -> x0, matrix products: 50.8 us -> none  [the longest x1 16.3 us: invert_frame(): jnp.dot(inverse_cols, matrix, preferred_element_type=jnp.float32)]
    another operation x2 -> x0, local copies, waits for them, and re-layouts: 49.3 us -> none  [column_matrix(): jnp.stack([upper, lower], axis=1).reshape(2 * length, 2 * length)]
  transfers between devices with their start and end apart: 3 -> 2, of which waited for: 3 -> 1; matrix products, arithmetic and copies ran while one was open for 22% -> 7% of each run, Pallas kernels for 0% -> 0%
where the time goes in v1:
time: 270 us; the launch traced here: 266 us
  waiting for transfers between devices  105 us (39%)
  blocking collectives  99.3 us (37%)
  Pallas kernels  34.6 us (13%)
  local copies, waits for them, and re-layouts  11.3 us (4%)
  starting transfers between devices  6.65 us (2%)
  other arithmetic  6.34 us (2%)
    ppermute x1, waiting for transfers between devices, on_device(): got = lax.ppermute(to_send, 'row', [(i, rows - 1 - i) for i in range(rows)])  105 us
    all_to_all x1, blocking collectives, on_device(): lax.all_to_all(back, ('gop', 'row'), split_axis=0, concat_axis=0, tiled=T...  99.3 us
    pallas_call x1, Pallas kernels, middle(): pl.pallas_call(functools.partial(middle_kernel, frames, rows, height), gr...  20.1 us
    dynamic_slice x2, local copies, waits for them, and re-layouts, on_device(): lax.dynamic_slice_in_dim(filters, start, WINDOW, 3)  9.34 us
    pallas_call x1, Pallas kernels, inverse_rows(): pl.pallas_call(functools.partial(inverse_kernel, block), grid=(h // block...  7.49 us
    pallas_call x1, Pallas kernels, forward_rows(): pl.pallas_call(functools.partial(forward_kernel, block), grid=(h // block...  7.01 us
    all_to_all x1, starting transfers between devices, on_device(): lax.all_to_all(done.reshape(devices, 2 * each, h, c), ('gop', 'row'), spl...  6.2 us
  transfers between devices with their start and end apart: 2, of which 1 were waited for; matrix products, arithmetic and copies ran while one was open for 7% of the time, Pallas kernels for 0%

profile of v1, /device:TPU:31, one launch (start us, length us, event | category | flops | bytes accessed | tf_op | source)
XLA Modules:
  0.0 266.0 jit_solution(10281609385397982908)
XLA Ops:
  0.0 7.0 %shard_map.73 = bf16[512,32,128]{2,1,0:T(8,128)(2,1)} custom-call(bf16[512,480]{1,0:T(8,128)(2,1)} %constant.47.clone.table_ref, bf16[32,480,128]{2,1,0:T(8,128)(2,1)} %bitcast.16), custom_call_target="tpu_custom_call" | custom-call | tf_op jit(solution)/shard_map/pallas_call | solution.py:66
  7.0 6.2 %all-to-all-start = ((bf16[32,16,32,128]{3,2,1,0:T(8,128)(2,1)}), bf16[32,16,32,128]{3,2,1,0:T(8,128)(2,1)}, u32[]{:S(2)}, u32[]{:S(2)}) async-start(bf16[32,16,32,128]{3,2,1,0:T(8,128)(2,1)} %bitcast.15), calls=%async_computation | async-start | bytes 8388608 | tf_op jit(solution)/shard_map/all_to_all | solution.py:243
  13.2 0.7 fusion.3
  15.3 0.6 fusion.2
  17.1 7.3 %constant_dynamic-slice_fusion = (bf16[3,256,2,8,128]{4,2,3,1,0:T(2,128)(2,1)S(1)}, bf16[3,256,2,8,128]{4,2,3,1,0:T(2,128)(2,1)S(1)}) fusion(bf16[3,256,2,60,128]{4,2,3,1,0:T(2,128)(2,1)} %param.8, s32[]{:T(128)S(6)} %select_n.32, s32[]{:T(128)S(6)} %select_n.31), kind=kLoop, calls=%fused_computation.12 | loop fusion | bytes 12582920 | tf_op jit(solution)/shard_map/dynamic_slice | solution.py:230
  24.3 0.0 copy-start
  24.4 2.1 copy.14
  26.4 0.5 collective-permute-start
  26.9 0.0 copy-done
  26.9 0.7 copy.10.anchor_ref
  27.6 0.6 add_clamp_fusion.place_ref
  28.1 0.6 add_convert_fusion.weight_ref
  28.7 105.2 %collective-permute-done = bf16[3,256,16,128]{3,2,1,0:T(8,128)(2,1)} collective-permute-done((bf16[3,256,16,128]{3,2,1,0:T(8,128)(2,1)}, bf16[3,256,16,128]{3,2,1,0:T(8,128)(2,1)}, u32[]{:S(2)}, u32[]{:S(2)}) %collective-permute-start) | collective-permute-done | bytes 3145760 | tf_op jit(solution)/shard_map/ppermute | solution.py:234
  133.9 5.2 %bitcast_select_fusion = (bf16[3,256,16,128]{3,2,1,0:T(8,128)(2,1)}, bf16[3,256,16,128]{3,2,1,0:T(8,128)(2,1)}) fusion(bf16[3,256,16,128]{3,2,1,0:T(8,128)(2,1)} %collective-permute-done, pred[]{:T(512)S(6)} %ge.13, bf16[3,256,2,8,128]{4,2,3,1,0:T(2,128)(2,1)S(1)} %get-tuple-element.5), kind=kLoop, calls=%fused_computation | loop fusion | flops 3145728 | bytes 12582913 | tf_op jit(solution)/shard_map/jit(_where)/select_n | solution.py:237
  139.1 0.0 all-to-all-done.x_ref
  139.1 20.1 %shard_map.74 = bf16[32,16,32,128]{3,2,1,0:T(8,128)(2,1)} custom-call(s32[2,8]{1,0:T(2,128)} %add_clamp_fusion.place_ref, f32[2,8]{1,0:T(2,128)} %add_convert_fusion.weight_ref, s32[4,2]{1,0:T(4,128)} %copy.10.anchor_ref, bf16[32,16,32,128]{3,2,1,0:T(8,128)(2,1)} %all-to-all-done.x_ref, bf16[3,256,16,128]{3,2,1,0:T(8,128)(2,1)} %get-tuple-element.8.p_ref, ...), custom_call_target="tpu_custom_call" | custom-call | tf_op jit(solution)/shard_map/pallas_call | solution.py:198
  159.1 99.3 %all_to_all.10 = bf16[32,16,32,128]{3,2,1,0:T(8,128)(2,1)} all-to-all(bf16[32,16,32,128]{3,2,1,0:T(8,128)(2,1)} %shard_map.74), channel_id=1, replica_groups=mesh['gop'=4,'row'=8] {'gop','row'}, dimensions={0} | all-to-all | bytes 8388608 | tf_op jit(solution)/shard_map/all_to_all | solution.py:250
  258.5 7.5 %shard_map.75 = bf16[32,480,128]{2,1,0:T(8,128)(2,1)} custom-call(bf16[480,512]{1,0:T(8,128)(2,1)} %constant.50.clone.table_ref, bf16[512,32,128]{2,1,0:T(8,128)(2,1)} %bitcast.14, bf16[32,480,128]{2,1,0:T(8,128)(2,1)} %bitcast.17), custom_call_target="tpu_custom_call" | custom-call | tf_op jit(solution)/shard_map/pallas_call | solution.py:97
  (4 shorter events, 0.0 us)
Async XLA Ops:
  7.0 132.1 %all-to-all-start = ((bf16[32,16,32,128]{3,2,1,0:T(8,128)(2,1)}), bf16[32,16,32,128]{3,2,1,0:T(8,128)(2,1)}, u32[]{:S(2)}, u32[]{:S(2)}) async-start(bf16[32,16,32,128]{3,2,1,0:T(8,128)(2,1)} %bitcast.15), calls=%async_computation | async-start | bytes 8388608 | tf_op jit(solution)/shard_map/all_to_all | solution.py:243
  24.3 2.5 copy-start
  26.4 107.5 %collective-permute-start = (bf16[3,256,16,128]{3,2,1,0:T(8,128)(2,1)}, bf16[3,256,16,128]{3,2,1,0:T(8,128)(2,1)}, u32[]{:S(2)}, u32[]{:S(2)}) collective-permute-start(bf16[3,256,16,128]{3,2,1,0:T(8,128)(2,1)} %bitcast.13), channel_id=1, source_target_pairs={{0,7},{1,6},{2,5},{3,4},{4,3},{5,2},{6,1},{7,0},{8,15},{9,14},{10,... | collective-permute-start | bytes 9437192 | tf_op jit(solution)/shard_map/ppermute | solution.py:234

commit v2 on v1

--- a/solution.py
+++ b/solution.py
@@ -10,8 +10,12 @@
 from jax.experimental.pallas import tpu as pltpu
 from jax.sharding import PartitionSpec as P
 
-WINDOW = 8
+CHUNKS = 2
 VMEM_LIMIT = 56 * 1024 * 1024
+
+
+def cost(flops, moved):
+    return pl.CostEstimate(flops=flops, bytes_accessed=moved, transcendentals=0)
 
 
 def trig(length, first, second):
@@ -73,13 +77,18 @@
         out_specs=pl.BlockSpec((count, block, c), lambda i: (0, i, 0)),
         out_shape=jax.ShapeDtypeStruct((count, h, c), jnp.bfloat16),
         scratch_shapes=[pltpu.VMEM((count * block, c), jnp.float32)],
+        cost_estimate=cost(2 * count * w * h * c, 2 * h * c * (w + count)),
         compiler_params=pltpu.CompilerParams(vmem_limit_bytes=VMEM_LIMIT),
     )(table, x)
 
 
-def inverse_kernel(rows_each, table_ref, b_ref, x_ref, o_ref, turned):
-    turned[...] = b_ref[...].reshape(turned.shape).astype(jnp.float32)
+def inverse_kernel(rows_each, chunks, table_ref, *refs):
+    b_refs, (x_ref, o_ref, turned) = refs[:chunks], refs[chunks:]
     count = table_ref.shape[1]
+    part = count // chunks * rows_each
+    for n in range(chunks):
+        wide = b_refs[n][...].reshape(part, 128).astype(jnp.float32)
+        turned[n * part : n * part + part, :] = wide
     for h in range(0, rows_each, 2):
         pair = jnp.concatenate(
             [turned[pl.ds(h + d, count, stride=rows_each), :] for d in range(2)], axis=1
@@ -90,44 +99,49 @@
             o_ref[h + d] = added.astype(jnp.bfloat16)
 
 
-def inverse_rows(table, back, x):
+def inverse_rows(table, backs, x):
     h, w, c = x.shape
     count = table.shape[1]
+    chunks = len(backs)
     block = 16
     return pl.pallas_call(
-        functools.partial(inverse_kernel, block),
+        functools.partial(inverse_kernel, block, chunks),
         grid=(h // block,),
         in_specs=[
             pl.BlockSpec((w, count), lambda i: (0, 0)),
-            pl.BlockSpec((count, block, c), lambda i: (0, i, 0)),
+            *[pl.BlockSpec((count // chunks, block, c), lambda i: (0, i, 0))] * chunks,
             pl.BlockSpec((block, w, c), lambda i: (i, 0, 0)),
         ],
         out_specs=pl.BlockSpec((block, w, c), lambda i: (i, 0, 0)),
         out_shape=jax.ShapeDtypeStruct((h, w, c), jnp.bfloat16),
         scratch_shapes=[pltpu.VMEM((count * block, c), jnp.float32)],
+        cost_estimate=cost(2 * count * w * h * c, 2 * h * c * (2 * w + count)),
         compiler_params=pltpu.CompilerParams(vmem_limit_bytes=VMEM_LIMIT),
-    )(table, back, x)
+    )(table, *backs, x)
 
 
 def middle_kernel(
-    frames, rows, height,
+    frames, rows, height, window,
     place_ref, weight_ref, anchor_ref, x_ref, p_ref, n_ref, mf_ref, mi_ref, o_ref,
-    p_wide, n_wide, spec, mixed,
+    p_wide, n_wide, n_plain, spec, mixed,
 ):
     slot = pl.program_id(0)
-    lines = 2 * WINDOW
+    lines = 2 * window
 
     @pl.when(slot == 0)
     def _():
-        def widen(k, carry):
-            mirror = lax.rem(height - k, height)
+        p_wide[...] = p_ref[...].astype(jnp.float32)
+        n_plain[...] = n_ref[...].astype(jnp.float32)
+
+        def mirror(k, carry):
+            there = lax.rem(height - k, height)
             for j in range(3):
-                at = pl.ds(pl.multiple_of((j * height + k) * lines, lines), lines)
-                p_wide[at, :] = p_ref[j, k].astype(jnp.float32)
-                n_wide[at, :] = n_ref[j, mirror].astype(jnp.float32)
+                to = pl.ds(pl.multiple_of((j * height + k) * lines, lines), lines)
+                at = pl.ds(pl.multiple_of((j * height + there) * lines, lines), lines)
+                n_wide[to, :] = n_plain[at, :]
             return carry
 
-        lax.fori_loop(0, height, widen, 0, unroll=4)
+        lax.fori_loop(0, height, mirror, 0, unroll=4)
 
     short = x_ref.shape[2]
     for f in range(0, frames, 2):
@@ -154,7 +168,7 @@
         for j in range(3):
             parts = []
             for p in range(2):
-                start = (j * height + k) * lines + p * WINDOW
+                start = (j * height + k) * lines + p * window
                 right = p_wide[pl.ds(start + place_p, chunk, stride=lines), :]
                 left = n_wide[pl.ds(start + place_n, chunk, stride=lines), :]
                 left = left * weight_n
@@ -189,25 +203,24 @@
                     o_ref[(f + d) * rows + r, q] = back[at : at + short, 128 * d : 128 * d + 128]
 
 
-def middle(frames, rows, place, weight, anchors, x, plus, minus, mf, mi):
+def middle(frames, rows, height, window, place, weight, anchors, x, plus, minus, mf, mi):
     n, count, short, c = x.shape
-    height = plus.shape[1]
     whole = lambda shape: pl.BlockSpec(shape, lambda i: (0,) * len(shape))
     smem = pl.BlockSpec(memory_space=pltpu.SMEM)
     block = pl.BlockSpec((n, 2, short, c), lambda i: (0, i, 0, 0))
     return pl.pallas_call(
-        functools.partial(middle_kernel, frames, rows, height),
+        functools.partial(middle_kernel, frames, rows, height, window),
         grid=(count // 2,),
         in_specs=[smem, smem, smem, block, whole(plus.shape), whole(minus.shape),
                   whole(mf.shape), whole(mi.shape)],
         out_specs=block,
         out_shape=jax.ShapeDtypeStruct(x.shape, jnp.bfloat16),
         scratch_shapes=[
-            pltpu.VMEM((3 * height * 2 * WINDOW, c), jnp.float32),
-            pltpu.VMEM((3 * height * 2 * WINDOW, c), jnp.float32),
+            *[pltpu.VMEM(plus.shape, jnp.float32)] * 3,
             pltpu.VMEM((frames, 2 * height, c), jnp.bfloat16),
             pltpu.VMEM((2 * height, frames * c), jnp.bfloat16),
         ],
+        cost_estimate=cost(8 * height * x.size, 4 * x.size + 4 * plus.size),
         compiler_params=pltpu.CompilerParams(vmem_limit_bytes=VMEM_LIMIT),
     )(place, weight, anchors, x, plus, minus, mf, mi)
 
@@ -222,34 +235,47 @@
     g, r = lax.axis_index("gop"), lax.axis_index("row")
     second = r >= rows // 2
 
-    slots = 2 * each * g + jnp.where(second, each, 0) + jnp.arange(each)
-    theirs = 2 * each * g + jnp.where(second, 0, each) + jnp.arange(each)
-    limit = per_row - WINDOW
+    chunks = math.gcd(CHUNKS, each)
+    size = each // chunks
+    window = max(4, size)
+    limit = per_row - window
     start_plus = lambda s: jnp.clip(s[0], 0, limit)
-    start_minus = lambda s: jnp.clip(per_row - s[each - 1], 0, limit)
-    cut = lambda start: lax.dynamic_slice_in_dim(filters, start, WINDOW, 3).reshape(
-        3, height, 2 * WINDOW, c
+    start_minus = lambda s: jnp.clip(per_row - s[size - 1], 0, limit)
+    cut = lambda start: lax.dynamic_slice_in_dim(filters, start, window, 3).reshape(-1, c)
+    tables = table.reshape(devices, chunks, 2 * size, w).swapaxes(0, 1).reshape(chunks, -1, w)
+    first_slot = 2 * each * g + jnp.where(second, each, 0)
+    first_theirs = 2 * each * g + jnp.where(second, 0, each)
+    forward = jnp.asarray(column_matrix(height, -1.0))
+    inverse = jnp.asarray(column_matrix(height, 1.0))
+    swap = lambda x: lax.all_to_all(
+        x.reshape(devices, 2 * size, h, c), ("gop", "row"), split_axis=0, concat_axis=0, tiled=True
     )
-    to_send = cut(jnp.where(second, start_minus(theirs), start_plus(theirs)))
-    got = lax.ppermute(to_send, "row", [(i, rows - 1 - i) for i in range(rows)])
-    own = cut(jnp.where(second, start_minus(slots), start_plus(slots)))
-    plus = jnp.where(second, got, own)
-    minus = jnp.where(second, own, got)
-    place = jnp.stack([slots - start_plus(slots), per_row - slots - start_minus(slots)])
-    place = jnp.clip(place, 0, WINDOW - 1).astype(jnp.int32)
-    weight = jnp.stack([slots < per_row, (slots >= 1) & (slots <= per_row)]).astype(jnp.float32)
-
-    done = forward_rows(jnp.asarray(table), features[0])
-    slab = lax.all_to_all(
-        done.reshape(devices, 2 * each, h, c), ("gop", "row"), split_axis=0, concat_axis=0, tiled=True
-    )
-    back = middle(
-        gops, rows, place, weight, anchors, slab, plus, minus,
-        jnp.asarray(column_matrix(height, -1.0)), jnp.asarray(column_matrix(height, 1.0)),
-    )
-    back = lax.all_to_all(back, ("gop", "row"), split_axis=0, concat_axis=0, tiled=True)
-    joined = inverse_rows(jnp.asarray(table.T), back.reshape(devices * 2 * each, h, c), features[0])
-    return joined[None]
+
+    gains, slabs = [], []
+    x = features[0]
+    for n in range(chunks):
+        slots = first_slot + n * size + jnp.arange(size)
+        theirs = first_theirs + n * size + jnp.arange(size)
+        to_send = cut(jnp.where(second, start_minus(theirs), start_plus(theirs)))
+        if n == 0:
+            x, to_send = lax.optimization_barrier((x, to_send))
+        got = lax.ppermute(to_send, "row", [(i, rows - 1 - i) for i in range(rows)])
+        own = cut(jnp.where(second, start_minus(slots), start_plus(slots)))
+        place = jnp.stack([slots - start_plus(slots), per_row - slots - start_minus(slots)])
+        place = jnp.clip(place, 0, window - 1).astype(jnp.int32)
+        weight = jnp.stack([slots < per_row, (slots >= 1) & (slots <= per_row)])
+        gains.append((place, weight.astype(jnp.float32), own, got))
+        slabs.append(swap(forward_rows(jnp.asarray(tables[n]), x)))
+    backs = []
+    for n in range(chunks):
+        place, weight, own, got = gains[n]
+        plus = jnp.where(second, got, own)
+        minus = jnp.where(second, own, got)
+        back = middle(gops, rows, height, window, place, weight, anchors, slabs[n], plus, minus,
+                      forward, inverse)
+        backs.append(swap(back).reshape(devices * 2 * size, h, c))
+    table_back = jnp.asarray(np.ascontiguousarray(tables.reshape(-1, w).T))
+    return inverse_rows(table_back, backs, features[0])[None]
 
 
 def solution(mesh):

time: 270 us -> 303 us (1.12)
  waiting for transfers between devices: 105 us -> 154 us
  blocking collectives: 99.3 us -> 52.5 us
  starting transfers between devices: 6.65 us -> 19 us
  local copies, waits for them, and re-layouts: 11.3 us -> 22 us
  Pallas kernels: 34.6 us -> 39.2 us
    all_to_all x1, blocking collectives: 99.3 us -> 52.5 us  [on_device(): lax.all_to_all(x.reshape(devices, 2 * size, h, c), ('gop', 'row'), split_...]
    all_to_all x1 -> x3, waiting for transfers between devices: 0.01 us -> 42.4 us  [on_device(): lax.all_to_all(x.reshape(devices, 2 * size, h, c), ('gop', 'row'), split_...]
    all_to_all x1 -> x3, starting transfers between devices: 6.2 us -> 18 us  [on_device(): lax.all_to_all(x.reshape(devices, 2 * size, h, c), ('gop', 'row'), split_...]
    dynamic_slice x2 -> x5, local copies, waits for them, and re-layouts: 9.34 us -> 16.3 us  [on_device(): lax.dynamic_slice_in_dim(filters, start, window, 3).reshape(-1, c)]
    ppermute x1 -> x2, waiting for transfers between devices: 105 us -> 111 us  [on_device(): got = lax.ppermute(to_send, 'row', [(i, rows - 1 - i) for i in range(rows)])]
    pallas_call x2 -> x3, Pallas kernels: 27.6 us -> 30 us  [the longest x2 22.5 us: middle(): pl.pallas_call(functools.partial(middle_kernel, frames, rows, height, win...]
    pallas_call x1 -> x2, Pallas kernels: 7.01 us -> 9.22 us  [forward_rows(): pl.pallas_call(functools.partial(forward_kernel, block), grid=(h // block...]
  transfers between devices with their start and end apart: 2 -> 5, of which waited for: 1 -> 3; matrix products, arithmetic and copies ran while one was open for 7% -> 5% of each run, Pallas kernels for 0% -> 9%
where the time goes in v2:
time: 303 us; the launch traced here: 299 us
  waiting for transfers between devices  154 us (51%)
  blocking collectives  52.5 us (17%)
  Pallas kernels  39.2 us (13%)
  local copies, waits for them, and re-layouts  22 us (7%)
  starting transfers between devices  19 us (6%)
  other arithmetic  7.85 us (3%)
  between operations  5.25 us (2%)
    ppermute x2, waiting for transfers between devices, on_device(): got = lax.ppermute(to_send, 'row', [(i, rows - 1 - i) for i in range(rows)])  111 us
    all_to_all x1, blocking collectives, on_device(): lax.all_to_all(x.reshape(devices, 2 * size, h, c), ('gop', 'row'), split_...  52.5 us
    all_to_all x3, waiting for transfers between devices, on_device(): lax.all_to_all(x.reshape(devices, 2 * size, h, c), ('gop', 'row'), split_...  42.4 us
    pallas_call x2, Pallas kernels, middle(): pl.pallas_call(functools.partial(middle_kernel, frames, rows, height, win...  22.5 us
    all_to_all x3, starting transfers between devices, on_device(): lax.all_to_all(x.reshape(devices, 2 * size, h, c), ('gop', 'row'), split_...  18 us
    dynamic_slice x5, local copies, waits for them, and re-layouts, on_device(): lax.dynamic_slice_in_dim(filters, start, window, 3).reshape(-1, c)  16.3 us
    pallas_call x2, Pallas kernels, forward_rows(): pl.pallas_call(functools.partial(forward_kernel, block), grid=(h // block...  9.22 us
    pallas_call x1, Pallas kernels, inverse_rows(): pl.pallas_call(functools.partial(inverse_kernel, block, chunks), grid=(h...  7.49 us
  transfers between devices with their start and end apart: 5, of which 3 were waited for; matrix products, arithmetic and copies ran while one was open for 5% of the time, Pallas kernels for 9%

profile of v2, /device:TPU:31, one launch (start us, length us, event | category | flops | bytes accessed | tf_op | source)
XLA Modules:
  0.0 299.3 jit_solution(3858212539300626377)
XLA Ops:
  0.0 0.6 fusion.5
  3.8 0.6 fusion.4
  7.6 7.7 %constant_dynamic-slice_fusion = (bf16[3,256,2,4,128]{4,2,3,1,0:T(2,128)(2,1)}, bf16[3,256,2,4,128]{4,2,3,1,0:T(2,128)(2,1)}, bf16[3,256,2,4,128]{4,2,3,1,0:T(2,128)(2,1)S(1)}, bf16[3,256,2,4,128]{4,2,3,1,0:T(2,128)(2,1)}) fusion(bf16[3,256,2,60,128]{4,2,3,1,0:T(2,128)(2,1)} %param.9, s32[]{:T(128)S(6)} %select_n.52, s32[]{:T(128)S(6)} %select_n.48, ...), kind=kLoop, calls=%fused_computation.10 | loop fusion | bytes 12582928 | tf_op jit(solution)/shard_map/dynamic_slice | solution.py:244
  15.3 1.7 copy.9
  17.0 4.6 %shard_map.84 = bf16[256,32,128]{2,1,0:T(8,128)(2,1)} custom-call(bf16[256,480]{1,0:T(8,128)(2,1)} %constant.64.clone.table_ref, bf16[32,480,128]{2,1,0:T(8,128)(2,1)} %bitcast.18), custom_call_target="tpu_custom_call" | custom-call | flops 1006632960 | bytes 6029312 | tf_op jit(solution)/shard_map/pallas_call | solution.py:70
  21.6 6.2 %all-to-all-start.2 = ((bf16[32,8,32,128]{3,2,1,0:T(8,128)(2,1)}), bf16[32,8,32,128]{3,2,1,0:T(8,128)(2,1)S(1)}, u32[]{:S(2)}, u32[]{:S(2)}) async-start(bf16[32,8,32,128]{3,2,1,0:T(8,128)(2,1)} %bitcast.22), calls=%async_computation.2 | async-start | bytes 4194304 | tf_op jit(solution)/shard_map/all_to_all | solution.py:250
  27.8 4.6 %shard_map.82 = bf16[256,32,128]{2,1,0:T(8,128)(2,1)} custom-call(bf16[256,480]{1,0:T(8,128)(2,1)} %constant.63.clone.table_ref, bf16[32,480,128]{2,1,0:T(8,128)(2,1)} %bitcast.19), custom_call_target="tpu_custom_call" | custom-call | flops 1006632960 | bytes 6029312 | tf_op jit(solution)/shard_map/pallas_call | solution.py:70
  32.4 42.4 %all-to-all-done.2.x_ref = bf16[32,8,32,128]{3,2,1,0:T(8,128)(2,1)S(1)} async-done(((bf16[32,8,32,128]{3,2,1,0:T(8,128)(2,1)}), bf16[32,8,32,128]{3,2,1,0:T(8,128)(2,1)S(1)}, u32[]{:S(2)}, u32[]{:S(2)}) %all-to-all-start.2) | async-done | bytes 2097184 | tf_op jit(solution)/shard_map/all_to_all | solution.py:250
  74.8 1.3 copy-done.1
  76.1 5.9 %all-to-all-start = ((bf16[32,8,32,128]{3,2,1,0:T(8,128)(2,1)}), bf16[32,8,32,128]{3,2,1,0:T(8,128)(2,1)S(1)}, u32[]{:S(2)}, u32[]{:S(2)}) async-start(bf16[32,8,32,128]{3,2,1,0:T(8,128)(2,1)} %bitcast.21), calls=%async_computation | async-start | bytes 4194304 | tf_op jit(solution)/shard_map/all_to_all | solution.py:250
  82.0 3.2 %copy.12 = bf16[3,256,2,4,128]{4,3,2,1,0:T(4,128)(2,1)} copy(bf16[3,256,2,4,128]{4,2,3,1,0:T(2,128)(2,1)} %get-tuple-element.12) | data formatting | bytes 3145728 | tf_op jit(solution)/shard_map/dynamic_slice | solution.py:244
  85.7 1.8 copy.13
  87.5 0.6 copy.11.anchor_ref
  89.2 53.9 %collective-permute-done.1 = bf16[6144,128]{1,0:T(8,128)(2,1)} collective-permute-done((bf16[6144,128]{1,0:T(8,128)(2,1)}, bf16[6144,128]{1,0:T(8,128)(2,1)}, u32[]{:S(2)}, u32[]{:S(2)}) %collective-permute-start.1) | collective-permute-done | bytes 1572896 | tf_op jit(solution)/shard_map/ppermute | solution.py:262
  143.1 3.7 %broadcast_select_fusion = (bf16[6144,128]{1,0:T(8,128)(2,1)}, bf16[6144,128]{1,0:T(8,128)(2,1)}) fusion(bf16[6144,128]{1,0:T(8,128)(2,1)} %bitcast.24, bf16[6144,128]{1,0:T(8,128)(2,1)} %collective-permute-done.1, pred[]{:T(512)S(6)} %ge.23), kind=kLoop, calls=%fused_computation | loop fusion | flops 1572864 | bytes 6291457 | tf_op jit(solution)/shard_map/jit(_where)/select_n | solution.py:273
  146.8 11.2 %shard_map.85 = bf16[32,8,32,128]{3,2,1,0:T(8,128)(2,1)} custom-call(s32[2,4]{1,0:T(2,128)} %add_clamp_fusion.1.place_ref, f32[2,4]{1,0:T(2,128)} %add_convert_fusion.1.weight_ref, s32[4,2]{1,0:T(4,128)} %copy.11.anchor_ref, bf16[32,8,32,128]{3,2,1,0:T(8,128)(2,1)} %copy-done.1, bf16[6144,128]{1,0:T(8,128)(2,1)} %get-tuple-element.14.p_ref, ...), custom_call_target="tpu_custom_call" | custom-call | flops 2147483648 | bytes 7340032 | tf_op jit(solution)/shard_map/pallas_call | solution.py:211
  158.0 1.3 copy-done
  159.3 5.9 %all-to-all-start.3 = ((bf16[32,8,32,128]{3,2,1,0:T(8,128)(2,1)}), bf16[32,8,32,128]{3,2,1,0:T(8,128)(2,1)}, u32[]{:S(2)}, u32[]{:S(2)}) async-start(bf16[32,8,32,128]{3,2,1,0:T(8,128)(2,1)} %shard_map.85), calls=%async_computation.3 | async-start | bytes 4194304 | tf_op jit(solution)/shard_map/all_to_all | solution.py:250
  165.8 1.9 copy.10
  168.9 57.3 %collective-permute-done = bf16[6144,128]{1,0:T(8,128)(2,1)S(1)} collective-permute-done((bf16[6144,128]{1,0:T(8,128)(2,1)}, bf16[6144,128]{1,0:T(8,128)(2,1)S(1)}, u32[]{:S(2)}, u32[]{:S(2)}) %collective-permute-start) | collective-permute-done | bytes 1572896 | tf_op jit(solution)/shard_map/ppermute | solution.py:262
  226.2 1.9 broadcast_select_fusion.2
  228.1 11.3 %shard_map.83 = bf16[32,8,32,128]{3,2,1,0:T(8,128)(2,1)} custom-call(s32[2,4]{1,0:T(2,128)} %add_clamp_fusion.place_ref, f32[2,4]{1,0:T(2,128)} %add_convert_fusion.weight_ref, s32[4,2]{1,0:T(4,128)} %copy.11.anchor_ref, bf16[32,8,32,128]{3,2,1,0:T(8,128)(2,1)} %copy-done, bf16[6144,128]{1,0:T(8,128)(2,1)} %get-tuple-element.16.p_ref, ...), custom_call_target="tpu_custom_call" | custom-call | flops 2147483648 | bytes 7340032 | tf_op jit(solution)/shard_map/pallas_call | solution.py:211
  239.4 52.5 %all_to_all.20 = bf16[32,8,32,128]{3,2,1,0:T(8,128)(2,1)} all-to-all(bf16[32,8,32,128]{3,2,1,0:T(8,128)(2,1)} %shard_map.83), channel_id=1, replica_groups=mesh['gop'=4,'row'=8] {'gop','row'}, dimensions={0} | all-to-all | bytes 4194304 | tf_op jit(solution)/shard_map/all_to_all | solution.py:250
  291.8 7.5 %shard_map.86 = bf16[32,480,128]{2,1,0:T(8,128)(2,1)} custom-call(bf16[480,512]{1,0:T(8,128)(2,1)} %constant.65.clone.table_ref, bf16[256,32,128]{2,1,0:T(8,128)(2,1)} %bitcast.23, bf16[256,32,128]{2,1,0:T(8,128)(2,1)} %bitcast.16.refs_1_, bf16[32,480,128]{2,1,0:T(8,128)(2,1)} %bitcast.20), custom_call_target="tpu_custom_call" | custom-call | flops 2013265920 | bytes 12058624 | tf_op jit(solution)/shard_map/pallas_call | solution.py:107
  (24 shorter events, 4.5 us)
Async XLA Ops:
  21.6 53.2 %all-to-all-start.2 = ((bf16[32,8,32,128]{3,2,1,0:T(8,128)(2,1)}), bf16[32,8,32,128]{3,2,1,0:T(8,128)(2,1)S(1)}, u32[]{:S(2)}, u32[]{:S(2)}) async-start(bf16[32,8,32,128]{3,2,1,0:T(8,128)(2,1)} %bitcast.22), calls=%async_computation.2 | async-start | bytes 4194304 | tf_op jit(solution)/shard_map/all_to_all | solution.py:250
  74.8 1.3 copy-start.1
  76.1 81.9 %all-to-all-start = ((bf16[32,8,32,128]{3,2,1,0:T(8,128)(2,1)}), bf16[32,8,32,128]{3,2,1,0:T(8,128)(2,1)S(1)}, u32[]{:S(2)}, u32[]{:S(2)}) async-start(bf16[32,8,32,128]{3,2,1,0:T(8,128)(2,1)} %bitcast.21), calls=%async_computation | async-start | bytes 4194304 | tf_op jit(solution)/shard_map/all_to_all | solution.py:250
  82.0 3.7 %copy-start.2 = (bf16[3,256,2,4,128]{4,2,3,1,0:T(2,128)(2,1)S(1)}, bf16[3,256,2,4,128]{4,2,3,1,0:T(2,128)(2,1)}, u32[]{:S(2)}) copy-start(bf16[3,256,2,4,128]{4,2,3,1,0:T(2,128)(2,1)} %get-tuple-element.9) | copy-start | bytes 4718596
  85.2 57.8 %collective-permute-start.1 = (bf16[6144,128]{1,0:T(8,128)(2,1)}, bf16[6144,128]{1,0:T(8,128)(2,1)}, u32[]{:S(2)}, u32[]{:S(2)}) collective-permute-start(bf16[6144,128]{1,0:T(8,128)(2,1)} %bitcast.14), channel_id=1, source_target_pairs={{0,7},{1,6},{2,5},{3,4},{4,3},{5,2},{6,1},{7,0},{8,15},{9,14},{10,... | collective-permute-start | bytes 4718600 | tf_op jit(solution)/shard_map/ppermute | solution.py:262
  85.7 1.8 copy-start.3
  158.0 1.3 copy-start
  159.3 80.0 %all-to-all-start.3 = ((bf16[32,8,32,128]{3,2,1,0:T(8,128)(2,1)}), bf16[32,8,32,128]{3,2,1,0:T(8,128)(2,1)}, u32[]{:S(2)}, u32[]{:S(2)}) async-start(bf16[32,8,32,128]{3,2,1,0:T(8,128)(2,1)} %shard_map.85), calls=%async_computation.3 | async-start | bytes 4194304 | tf_op jit(solution)/shard_map/all_to_all | solution.py:250
  165.3 60.9 %collective-permute-start = (bf16[6144,128]{1,0:T(8,128)(2,1)}, bf16[6144,128]{1,0:T(8,128)(2,1)S(1)}, u32[]{:S(2)}, u32[]{:S(2)}) collective-permute-start(bf16[6144,128]{1,0:T(8,128)(2,1)} %bitcast.26), channel_id=1, source_target_pairs={{0,7},{1,6},{2,5},{3,4},{4,3},{5,2},{6,1},{7,0},{8,15},{9,14},{10,... | collective-permute-start | bytes 4718600 | tf_op jit(solution)/shard_map/ppermute | solution.py:262

commit v3 on v1

v3 whole, which is shorter than its diff:
```python
import functools
import math

import jax
import jax.numpy as jnp
import ml_dtypes
import numpy as np
from jax import lax
from jax.experimental import pallas as pl
from jax.experimental.pallas import tpu as pltpu
from jax.sharding import PartitionSpec as P

CHUNKS = 4
MESH = pl.DeviceIdType.MESH
VMEM_LIMIT = 56 * 1024 * 1024


def cost(flops, moved):
    return pl.CostEstimate(flops=flops, bytes_accessed=moved, transcendentals=0)


def trig(length, first, second):
    phases = (first[:, None].astype(np.int64) * second[None, :]) % length
    angles = phases.astype(np.float32) * np.float32(2.0 * math.pi / length)
    factor = np.float32(1.0 / math.sqrt(length))
    return np.cos(angles) * factor, np.sin(angles) * factor


def layout(gops, rows, width):
    per_row = width // rows
    each = -(-(per_row + 1) // (2 * gops))
    columns = []
    for g in range(gops):
        for r in range(rows):
            second = r >= rows // 2
            pair = rows - 1 - r if second else r
            for i in range(each):
                s = 2 * each * g + (each if second else 0) + i
                columns.append(per_row * pair + s if s <= per_row else -1)
    return each, np.array(columns)


def row_rows(gops, rows, width):
    each, columns = layout(gops, rows, width)
    cosine, sine = trig(width, np.maximum(columns, 0), np.arange(width))
    table = np.stack([cosine, -sine], axis=1) * (columns >= 0)[:, None, None]
    return table.reshape(2 * len(columns), width).astype(ml_dtypes.bfloat16)


def column_matrix(length, sign):
    across = np.arange(length)
    cosine, sine = trig(length, across, across)
    sine = np.float32(sign) * sine
    return np.block([[cosine, -sine], [sine, cosine]]).astype(ml_dtypes.bfloat16)


def inverse_kernel(rows_each, table_ref, b_ref, x_ref, o_ref, turned):
    turned[...] = b_ref[...].reshape(turned.shape).astype(jnp.float32)
    count = table_ref.shape[1]
    for h in range(0, rows_each, 2):
        pair = jnp.concatenate(
            [turned[pl.ds(h + d, count, stride=rows_each), :] for d in range(2)], axis=1
        ).astype(jnp.bfloat16)
        done = jnp.dot(table_ref[...], pair, preferred_element_type=jnp.float32)
        for d in range(2):
            added = x_ref[h + d].astype(jnp.float32) + done[:, 128 * d : 128 * d + 128]
            o_ref[h + d] = added.astype(jnp.bfloat16)


def inverse_rows(table, back, x):
    h, w, c = x.shape
    count = table.shape[1]
    block = 16
    return pl.pallas_call(
        functools.partial(inverse_kernel, block),
        grid=(h // block,),
        in_specs=[
            pl.BlockSpec((w, count), lambda i: (0, 0)),
            pl.BlockSpec((count, block, c), lambda i: (0, i, 0)),
            pl.BlockSpec((block, w, c), lambda i: (i, 0, 0)),
        ],
        out_specs=pl.BlockSpec((block, w, c), lambda i: (i, 0, 0)),
        out_shape=jax.ShapeDtypeStruct((h, w, c), jnp.bfloat16),
        scratch_shapes=[pltpu.VMEM((count * block, c), jnp.float32)],
        cost_estimate=cost(2 * count * w * h * c, 2 * h * c * (2 * w + count)),
        compiler_params=pltpu.CompilerParams(vmem_limit_bytes=VMEM_LIMIT),
    )(table, back, x)


def exchange_kernel(
    frames, rows, height, chunks, size, parts, fold, window,
    place_ref, weight_ref, anchor_ref, table_ref, x_ref, own_ref, give_ref, mf_ref, mi_ref, o_ref,
    turned, sent, slab, back, got, p_wide, n_wide, n_plain, spec, mixed,
    f_send, f_recv, a_send, a_recv, b_send, b_recv, local_sem,
):
    devices = frames * rows
    g, r = lax.axis_index("gop"), lax.axis_index("row")
    me = g * rows + r
    second = r >= rows // 2
    short = x_ref.shape[0]
    lines = 2 * window

    def target(step):
        to = lax.rem(me + step, devices)
        return to, (to // rows, lax.rem(to, rows))

    barrier = pltpu.get_barrier_semaphore()

    def greet(step, carry):
        _, there = target(step)
        pl.semaphore_signal(barrier, inc=1, device_id=there, device_id_type=MESH)
        return carry

    lax.fori_loop(1, devices, greet, 0)
    pl.semaphore_wait(barrier, devices - 1)

    def gain_copy(part):
        return pltpu.make_async_remote_copy(
            src_ref=give_ref.at[part], dst_ref=got.at[part],
            send_sem=f_send.at[part], recv_sem=f_recv.at[part],
            device_id=(g, rows - 1 - r), device_id_type=MESH,
        )

    for part in range(parts):
        gain_copy(part).start()

    def send_all(n, source, landing, send_sem, recv_sem):
        def one(step, carry):
            to, there = target(step)
            pltpu.make_async_remote_copy(
                src_ref=source.at[n, to], dst_ref=landing.at[n, me],
                send_sem=send_sem.at[n], recv_sem=recv_sem.at[n],
                device_id=there, device_id_type=MESH,
            ).start()
            return carry

        lax.fori_loop(1, devices, one, 0)

    def wait_all(n, ref, sem):
        some = ref.at[n, pl.ds(0, devices - 1)]
        pltpu.make_async_copy(some, some, sem.at[n]).wait()

    count = devices * size * 2

    def forward(n, carry):
        for half in range(short // 16):
            def two(i, inner):
                h = half * 16 + 2 * i
                pair = jnp.concatenate([x_ref[h], x_ref[h + 1]], axis=1)
                done = jnp.dot(table_ref[n], pair, preferred_element_type=jnp.float32)
                turned[pl.ds(2 * i, count, stride=16), :] = done[:, :128]
                turned[pl.ds(2 * i + 1, count, stride=16), :] = done[:, 128:]
                return inner

            lax.fori_loop(0, 8, two, 0, unroll=True)
            sent[n, :, :, pl.ds(half * 16, 16), :] = (
                turned[...].astype(jnp.bfloat16).reshape(devices, 2 * size, 16, 128)
            )
        send_all(n, sent, slab, a_send, a_recv)
        slab[n, me] = sent[n, me]
        return carry

    lax.fori_loop(0, chunks, forward, 0)

    def middle(n, carry):
        @pl.when(lax.rem(n, fold) == 0)
        def _():
            part = n // fold
            gain_copy(part).wait()
            block = 512

            def widen(i, inner):
                at = pl.ds(pl.multiple_of(i * block, block), block)
                own = own_ref[part, at, :].astype(jnp.float32)
                other = got[part, at, :].astype(jnp.float32)
                p_wide[at, :] = jnp.where(second, other, own)
                n_plain[at, :] = jnp.where(second, own, other)
                return inner

            lax.fori_loop(0, 3 * height * lines // block, widen, 0)

            def mirror(k, inner):
                there = lax.rem(height - k, height)
                for j in range(3):
                    to = pl.ds(pl.multiple_of((j * height + k) * lines, lines), lines)
                    at = pl.ds(pl.multiple_of((j * height + there) * lines, lines), lines)
                    n_wide[to, :] = n_plain[at, :]
                return inner

            lax.fori_loop(0, height, mirror, 0)

        wait_all(n, slab, a_recv)

        def one_slot(i, inner):
            slot = n * size + i
            for f in range(0, frames, 2):
                sides = [
                    jnp.concatenate(
                        [slab[n, (f + d) * rows + k, 2 * i + q] for q in range(2) for k in range(rows)],
                        axis=0,
                    )
                    for d in range(2)
                ]
                done = jnp.dot(
                    mf_ref[...], jnp.concatenate(sides, axis=1), preferred_element_type=jnp.float32
                ).astype(jnp.bfloat16)
                spec[f] = done[:, :128]
                spec[f + 1] = done[:, 128:]

            place_p, place_n = place_ref[0, slot], place_ref[1, slot]
            weight_p, weight_n = weight_ref[0, slot], weight_ref[1, slot]
            chunk = 32

            def mix(step, deep):
                k = pl.multiple_of(step * chunk, chunk)
                gains = []
                for j in range(3):
                    pieces = []
                    for p in range(2):
                        start = (j * height + k) * lines + p * window
                        right = p_wide[pl.ds(start + place_p, chunk, stride=lines), :]
                        left = n_wide[pl.ds(start + place_n, chunk, stride=lines), :]
                        left = left * weight_n
                        pieces.append(right * weight_p + (left if p == 0 else -left))
                    gains.append(pieces)
                for f in range(frames):
                    real, imag = None, None
                    for j in range(3):
                        source = f if j == 0 else anchor_ref[f, j - 1]
                        s_real = spec[source, pl.ds(k, chunk), :].astype(jnp.float32)
                        s_imag = spec[source, pl.ds(height + k, chunk), :].astype(jnp.float32)
                        g_real, g_imag = gains[j]
                        new_real = g_real * s_real - g_imag * s_imag
                        new_imag = g_real * s_imag + g_imag * s_real
                        real = new_real if real is None else real + new_real
                        imag = new_imag if imag is None else imag + new_imag
                    lanes = pl.ds(f * 128, 128)
                    mixed[pl.ds(k, chunk), lanes] = real.astype(jnp.bfloat16)
                    mixed[pl.ds(height + k, chunk), lanes] = imag.astype(jnp.bfloat16)
                return deep

            lax.fori_loop(0, height // chunk, mix, 0)

            for f in range(0, frames, 2):
                done = jnp.dot(
                    mi_ref[...], mixed[:, 128 * f : 128 * f + 256],
                    preferred_element_type=jnp.float32,
                ).astype(jnp.bfloat16)
                for d in range(2):
                    for q in range(2):
                        for k in range(rows):
                            at = q * height + k * short
                            back[n, (f + d) * rows + k, 2 * i + q] = done[
                                at : at + short, 128 * d : 128 * d + 128
                            ]
            return inner

        lax.fori_loop(0, size, one_slot, 0)
        send_all(n, back, o_ref, b_send, b_recv)
        pltpu.make_async_copy(back.at[n, me], o_ref.at[n, me], local_sem.at[n]).start()
        return carry

    lax.fori_loop(0, chunks, middle, 0)

    def finish(n, carry):
        wait_all(n, sent, a_send)
        wait_all(n, back, b_send)
        wait_all(n, o_ref, b_recv)
        pltpu.make_async_copy(back.at[n, me], o_ref.at[n, me], local_sem.at[n]).wait()
        return carry

    lax.fori_loop(0, chunks, finish, 0)


def exchange(frames, rows, height, size, fold, window, place, weight, anchors, table, x, own, give, mf, mi):
    chunks, count, w = table.shape
    h, _, c = x.shape
    devices = frames * rows
    parts = own.shape[0]
    shape = (chunks, devices, 2 * size, h, c)
    smem = pl.BlockSpec(memory_space=pltpu.SMEM)
    vmem = pl.BlockSpec(memory_space=pltpu.VMEM)
    hbm = pl.BlockSpec(memory_space=pl.ANY)
    wide = pltpu.VMEM(own.shape[1:], jnp.float32)
    dma = pltpu.SemaphoreType.DMA
    return pl.pallas_call(
        functools.partial(exchange_kernel, frames, rows, height, chunks, size, parts, fold, window),
        in_specs=[smem, smem, smem, vmem, vmem, vmem, hbm, vmem, vmem],
        out_specs=hbm,
        out_shape=jax.ShapeDtypeStruct(shape, jnp.bfloat16),
        scratch_shapes=[
            pltpu.VMEM((count * 16, c), jnp.float32),
            *[pltpu.VMEM(shape, jnp.bfloat16)] * 3,
            pltpu.VMEM(own.shape, jnp.bfloat16),
            wide, wide, wide,
            pltpu.VMEM((frames, 2 * height, c), jnp.bfloat16),
            pltpu.VMEM((2 * height, frames * c), jnp.bfloat16),
            dma((parts,)), dma((parts,)),
            *[dma((chunks,))] * 5,
        ],
        cost_estimate=cost(8 * height * x.size, 4 * x.size + 4 * own.size),
        compiler_params=pltpu.CompilerParams(
            vmem_limit_bytes=VMEM_LIMIT, collective_id=0, has_side_effects=True
        ),
    )(place, weight, anchors, table, x, own, give, mf, mi)


def on_device(gops, rows, features, filters, anchors):
    h, w, c = features.shape[1:]
    height = filters.shape[1]
    per_row = filters.shape[3]
    devices = gops * rows
    table = row_rows(gops, rows, w)
    each, _ = layout(gops, rows, w)
    g, r = lax.axis_index("gop"), lax.axis_index("row")
    second = r >= rows // 2
    window = 4
    parts = max(1, each // window)
    part_size = each // parts
    chunks = math.gcd(CHUNKS, each)
    size = each // chunks
    limit = per_row - window
    start_plus = lambda s: jnp.clip(s[0], 0, limit)
    start_minus = lambda s: jnp.clip(per_row - s[part_size - 1], 0, limit)
    cut = lambda start: lax.dynamic_slice_in_dim(filters, start, window, 3).reshape(-1, c)
    tables = table.reshape(devices, chunks, 2 * size, w).swapaxes(0, 1).reshape(chunks, -1, w)
    first_slot = 2 * each * g + jnp.where(second, each, 0)
    first_theirs = 2 * each * g + jnp.where(second, 0, each)

    give, own, places, weights = [], [], [], []
    for n in range(parts):
        slots = first_slot + n * part_size + jnp.arange(part_size)
        theirs = first_theirs + n * part_size + jnp.arange(part_size)
        give.append(cut(jnp.where(second, start_minus(theirs), start_plus(theirs))))
        own.append(cut(jnp.where(second, start_minus(slots), start_plus(slots))))
        places.append(jnp.stack([slots - start_plus(slots), per_row - slots - start_minus(slots)]))
        weights.append(jnp.stack([slots < per_row, (slots >= 1) & (slots <= per_row)]))
    place = jnp.clip(jnp.concatenate(places, axis=1), 0, window - 1).astype(jnp.int32)
    weight = jnp.concatenate(weights, axis=1).astype(jnp.float32)
    back = exchange(
        gops, rows, height, size, part_size // size, window, place, weight, anchors,
        jnp.asarray(tables), features[0], jnp.stack(own), jnp.stack(give),
        jnp.asarray(column_matrix(height, -1.0)), jnp.asarray(column_matrix(height, 1.0)),
    )
    table_back = jnp.asarray(np.ascontiguousarray(tables.reshape(-1, w).T))
    return inverse_rows(table_back, back.reshape(-1, h, c), features[0])[None]


def solution(mesh):
    in_specs = (P("gop", "row", None, None), P(None, None, None, "row", None), P())
    out_specs = P("gop", "row", None, None)
    return jax.shard_map(
        functools.partial(on_device, mesh.shape["gop"], mesh.shape["row"]),
        mesh=mesh, in_specs=in_specs, out_specs=out_specs, check_vma=False,
    )
```

time: 270 us -> 251 us (0.930); the launches traced: 266 us -> 251 us
  Pallas kernels: 34.6 us -> 230 us
  waiting for transfers between devices: 105 us -> 0 us
  blocking collectives: 99.3 us -> 0 us
  starting transfers between devices: 6.65 us -> 0 us
    pallas_call x2 -> x1, Pallas kernels: 27.1 us -> 222 us  [exchange(): pl.pallas_call(functools.partial(exchange_kernel, frames, rows, height, c...]
    ppermute x1 -> x0, waiting for transfers between devices: 105 us -> none  [on_device(): got = lax.ppermute(to_send, 'row', [(i, rows - 1 - i) for i in range(rows)])]
    all_to_all x1 -> x0, blocking collectives: 99.3 us -> none  [on_device(): lax.all_to_all(back, ('gop', 'row'), split_axis=0, concat_axis=0, tiled=T...]
    all_to_all x1 -> x0, starting transfers between devices: 6.2 us -> none  [on_device(): lax.all_to_all(done.reshape(devices, 2 * each, h, c), ('gop', 'row'), spl...]
    select_n x1 -> x0, other arithmetic: 5.16 us -> none  [on_device(): minus = jnp.where(second, own, got)]
    another operation x0 -> x1, other arithmetic: none -> 3.02 us  [on_device(): jnp.stack(own)]
    dynamic_slice x2 -> x5, local copies, waits for them, and re-layouts: 9.34 us -> 8.31 us  [on_device(): lax.dynamic_slice_in_dim(filters, start, window, 3).reshape(-1, c)]
  transfers between devices with their start and end apart: 2 -> 0, of which waited for: 1 -> 0; matrix products, arithmetic and copies ran while one was open for 7% -> 0% of each run, Pallas kernels for 0% -> 0%
where the time goes in v3:
time: 251 us
  Pallas kernels  230 us (92%)
  local copies, waits for them, and re-layouts  11.4 us (5%)
  between operations  5.28 us (2%)
  other arithmetic  4.38 us (2%)
    pallas_call x1, Pallas kernels, exchange(): pl.pallas_call(functools.partial(exchange_kernel, frames, rows, height, c...  222 us
    dynamic_slice x5, local copies, waits for them, and re-layouts, on_device(): lax.dynamic_slice_in_dim(filters, start, window, 3).reshape(-1, c)  8.31 us
    pallas_call x1, Pallas kernels, inverse_rows(): pl.pallas_call(functools.partial(inverse_kernel, block), grid=(h // block...  7.52 us

profile of v3, /device:TPU:31, one launch (start us, length us, event | category | flops | bytes accessed | tf_op | source)
XLA Modules:
  0.0 250.8 jit_solution(2225202609147026109)
XLA Ops:
  0.0 0.6 fusion.7
  1.9 0.6 fusion.6
  3.8 0.6 fusion.5
  5.8 0.6 fusion.4
  7.7 6.1 %constant_dynamic-slice_fusion.1 = (bf16[3,256,2,4,128]{4,2,3,1,0:T(2,128)(2,1)S(1)}, bf16[3,256,2,4,128]{4,2,3,1,0:T(2,128)(2,1)S(1)}, bf16[3,256,2,4,128]{4,2,...) fusion(bf16[3,256,2,60,128]{4,2,3,1,0:T(2,128)(2,1)} %param.8, s32[]{:T(128)S(6)} %select_n.28, s32[]{:T(128)S(6)} %select_n.26, ...), kind=kLoop, calls=%fused_computation.7 | loop fusion | bytes 12582928 | tf_op jit(solution)/shard_map/dynamic_slice | solution.py:325
  13.8 0.5 copy.11
  14.4 0.5 copy.8
  14.9 0.5 copy.9
  15.5 0.5 copy.10
  16.0 0.0 copy-start
  16.0 3.0 %pad_maximum_fusion = (bf16[2,6144,128]{2,1,0:T(8,128)(2,1)}, bf16[2,6144,128]{2,1,0:T(8,128)(2,1)}) fusion(bf16[1,6144,128]{2,1,0:T(8,128)(2,1)S(1)} %bitcast.20, bf16[1,6144,128]{2,1,0:T(8,128)(2,1)S(1)} %bitcast.19, bf16[1,6144,128]{2,1,0:T(8,128)(2,1)S(1)} %bitcast.18, bf16[1,6144,128]{2,1,0:T(8,128)(2,1)S(1)} %bitcast.21), kind=kLoop, calls=%fused_computation | loop fusion | flops 3145728 | bytes 12582912 | tf_op jit(solution)/shard_map/stack | solution.py:342
  19.1 0.7 add_clamp_fusion.place_ref
  19.8 0.7 add_convert_fusion.weight_ref
  20.4 0.0 copy-done
  20.4 0.7 copy.12.anchor_ref
  21.1 222.2 %shard_map.73 = bf16[4,32,4,32,128]{4,3,2,1,0:T(8,128)(2,1)} custom-call(s32[2,8]{1,0:T(2,128)} %add_clamp_fusion.place_ref, f32[2,8]{1,0:T(2,128)} %add_convert_fusion.weight_ref, s32[4,2]{1,0:T(4,128)} %copy.12.anchor_ref, bf16[4,128,480]{2,1,0:T(8,128)(2,1)} %constant.59.clone.table_ref, bf16[32,480,128]{2,1,0:T(8,128)(2,1)} %bitcast.16, ...), custom_call_target="tpu_custom_call" | custom-call | flops 4026531840 | bytes 14155776 | tf_op jit(solution)/shard_map/pallas_call | solution.py:286
  243.3 7.5 %shard_map.74 = bf16[32,480,128]{2,1,0:T(8,128)(2,1)} custom-call(bf16[480,512]{1,0:T(8,128)(2,1)} %constant.62.clone.table_ref, bf16[512,32,128]{2,1,0:T(8,128)(2,1)} %bitcast.15, bf16[32,480,128]{2,1,0:T(8,128)(2,1)} %bitcast.17), custom_call_target="tpu_custom_call" | custom-call | flops 2013265920 | bytes 12058624 | tf_op jit(solution)/shard_map/pallas_call | solution.py:74
  (8 shorter events, 0.0 us)
Async XLA Ops:
  16.0 4.4 %copy-start = (s32[4,2]{0,1:T(2,128)S(1)}, s32[4,2]{0,1:T(2,128)}, u32[]{:S(2)}) copy-start(s32[4,2]{0,1:T(2,128)} %param.9) | copy-start | bytes 100

commit v4 on v3

--- a/solution.py
+++ b/solution.py
@@ -11,6 +11,7 @@
 from jax.sharding import PartitionSpec as P
 
 CHUNKS = 4
+STRIDE = 13
 MESH = pl.DeviceIdType.MESH
 VMEM_LIMIT = 56 * 1024 * 1024
 
@@ -89,10 +90,13 @@
 
 def exchange_kernel(
     frames, rows, height, chunks, size, parts, fold, window,
-    place_ref, weight_ref, anchor_ref, table_ref, x_ref, own_ref, give_ref, mf_ref, mi_ref, o_ref,
-    turned, sent, slab, back, got, p_wide, n_wide, n_plain, spec, mixed,
-    f_send, f_recv, a_send, a_recv, b_send, b_recv, local_sem,
+    place_ref, anchor_ref, table_ref, x_ref, mf_ref, mi_ref, *refs,
 ):
+    own_refs, give_refs, refs = refs[:parts], refs[parts : 2 * parts], refs[2 * parts :]
+    (
+        o_ref, turned, sent, slab, back, got, p_wide, n_wide, n_plain, spec, mixed,
+        f_send, f_recv, a_send, a_recv, b_send, b_recv, local_sem,
+    ) = refs
     devices = frames * rows
     g, r = lax.axis_index("gop"), lax.axis_index("row")
     me = g * rows + r
@@ -101,7 +105,7 @@
     lines = 2 * window
 
     def target(step):
-        to = lax.rem(me + step, devices)
+        to = lax.rem(me + step * STRIDE, devices)
         return to, (to // rows, lax.rem(to, rows))
 
     barrier = pltpu.get_barrier_semaphore()
@@ -112,17 +116,13 @@
         return carry
 
     lax.fori_loop(1, devices, greet, 0)
-    pl.semaphore_wait(barrier, devices - 1)
 
     def gain_copy(part):
         return pltpu.make_async_remote_copy(
-            src_ref=give_ref.at[part], dst_ref=got.at[part],
+            src_ref=give_refs[part], dst_ref=got.at[part],
             send_sem=f_send.at[part], recv_sem=f_recv.at[part],
             device_id=(g, rows - 1 - r), device_id_type=MESH,
         )
-
-    for part in range(parts):
-        gain_copy(part).start()
 
     def send_all(n, source, landing, send_sem, recv_sem):
         def one(step, carry):
@@ -142,7 +142,7 @@
 
     count = devices * size * 2
 
-    def forward(n, carry):
+    def forward(n):
         for half in range(short // 16):
             def two(i, inner):
                 h = half * 16 + 2 * i
@@ -156,38 +156,53 @@
             sent[n, :, :, pl.ds(half * 16, 16), :] = (
                 turned[...].astype(jnp.bfloat16).reshape(devices, 2 * size, 16, 128)
             )
+
+    def send_forward(n):
         send_all(n, sent, slab, a_send, a_recv)
         slab[n, me] = sent[n, me]
+
+    def later(n, carry):
+        forward(n)
+        send_forward(n)
         return carry
 
-    lax.fori_loop(0, chunks, forward, 0)
+    forward(0)
+    pl.semaphore_wait(barrier, devices - 1)
+    for part in range(parts):
+        gain_copy(part).start()
+        if part == 0:
+            send_forward(0)
+        lax.fori_loop(max(1, part * fold), (part + 1) * fold, later, 0)
+
+    def load_gains(part):
+        gain_copy(part).wait()
+        block = 512
+
+        def widen(i, carry):
+            at = pl.ds(pl.multiple_of(i * block, block), block)
+            own = own_refs[part][at, :].astype(jnp.float32)
+            other = got[part, at, :].astype(jnp.float32)
+            p_wide[at, :] = jnp.where(second, other, own)
+            n_plain[at, :] = jnp.where(second, own, other)
+            return carry
+
+        lax.fori_loop(0, 3 * height * lines // block, widen, 0)
+
+        def mirror(k, carry):
+            there = lax.rem(height - k, height)
+            for j in range(3):
+                to = pl.ds(pl.multiple_of((j * height + k) * lines, lines), lines)
+                at = pl.ds(pl.multiple_of((j * height + there) * lines, lines), lines)
+                n_wide[to, :] = n_plain[at, :]
+            return carry
+
+        lax.fori_loop(0, height, mirror, 0)
 
     def middle(n, carry):
-        @pl.when(lax.rem(n, fold) == 0)
-        def _():
-            part = n // fold
-            gain_copy(part).wait()
-            block = 512
-
-            def widen(i, inner):
-                at = pl.ds(pl.multiple_of(i * block, block), block)
-                own = own_ref[part, at, :].astype(jnp.float32)
-                other = got[part, at, :].astype(jnp.float32)
-                p_wide[at, :] = jnp.where(second, other, own)
-                n_plain[at, :] = jnp.where(second, own, other)
-                return inner
-
-            lax.fori_loop(0, 3 * height * lines // block, widen, 0)
-
-            def mirror(k, inner):
-                there = lax.rem(height - k, height)
-                for j in range(3):
-                    to = pl.ds(pl.multiple_of((j * height + k) * lines, lines), lines)
-                    at = pl.ds(pl.multiple_of((j * height + there) * lines, lines), lines)
-                    n_wide[to, :] = n_plain[at, :]
-                return inner
-
-            lax.fori_loop(0, height, mirror, 0)
+        for part in range(parts):
+            @pl.when(n == part * fold)
+            def _():
+                load_gains(part)
 
         wait_all(n, slab, a_recv)
 
@@ -208,7 +223,8 @@
                 spec[f + 1] = done[:, 128:]
 
             place_p, place_n = place_ref[0, slot], place_ref[1, slot]
-            weight_p, weight_n = weight_ref[0, slot], weight_ref[1, slot]
+            weight_p = place_ref[2, slot].astype(jnp.float32)
+            weight_n = place_ref[3, slot].astype(jnp.float32)
             chunk = 32
 
             def mix(step, deep):
@@ -272,37 +288,37 @@
     lax.fori_loop(0, chunks, finish, 0)
 
 
-def exchange(frames, rows, height, size, fold, window, place, weight, anchors, table, x, own, give, mf, mi):
+def exchange(frames, rows, height, size, fold, window, place, anchors, table, x, own, give, mf, mi):
     chunks, count, w = table.shape
     h, _, c = x.shape
     devices = frames * rows
-    parts = own.shape[0]
+    parts = len(own)
     shape = (chunks, devices, 2 * size, h, c)
     smem = pl.BlockSpec(memory_space=pltpu.SMEM)
     vmem = pl.BlockSpec(memory_space=pltpu.VMEM)
     hbm = pl.BlockSpec(memory_space=pl.ANY)
-    wide = pltpu.VMEM(own.shape[1:], jnp.float32)
+    wide = pltpu.VMEM(own[0].shape, jnp.float32)
     dma = pltpu.SemaphoreType.DMA
     return pl.pallas_call(
         functools.partial(exchange_kernel, frames, rows, height, chunks, size, parts, fold, window),
-        in_specs=[smem, smem, smem, vmem, vmem, vmem, hbm, vmem, vmem],
+        in_specs=[smem, smem, vmem, vmem, vmem, vmem, *[vmem] * parts, *[hbm] * parts],
         out_specs=hbm,
         out_shape=jax.ShapeDtypeStruct(shape, jnp.bfloat16),
         scratch_shapes=[
             pltpu.VMEM((count * 16, c), jnp.float32),
             *[pltpu.VMEM(shape, jnp.bfloat16)] * 3,
-            pltpu.VMEM(own.shape, jnp.bfloat16),
+            pltpu.VMEM((parts, *own[0].shape), jnp.bfloat16),
             wide, wide, wide,
             pltpu.VMEM((frames, 2 * height, c), jnp.bfloat16),
             pltpu.VMEM((2 * height, frames * c), jnp.bfloat16),
             dma((parts,)), dma((parts,)),
             *[dma((chunks,))] * 5,
         ],
-        cost_estimate=cost(8 * height * x.size, 4 * x.size + 4 * own.size),
+        cost_estimate=cost(8 * height * x.size, 4 * x.size + 4 * parts * own[0].size),
         compiler_params=pltpu.CompilerParams(
             vmem_limit_bytes=VMEM_LIMIT, collective_id=0, has_side_effects=True
         ),
-    )(place, weight, anchors, table, x, own, give, mf, mi)
+    )(place, anchors, table, x, mf, mi, *own, *give)
 
 
 def on_device(gops, rows, features, filters, anchors):
@@ -320,26 +336,32 @@
     chunks = math.gcd(CHUNKS, each)
     size = each // chunks
     limit = per_row - window
-    start_plus = lambda s: jnp.clip(s[0], 0, limit)
-    start_minus = lambda s: jnp.clip(per_row - s[part_size - 1], 0, limit)
     cut = lambda start: lax.dynamic_slice_in_dim(filters, start, window, 3).reshape(-1, c)
     tables = table.reshape(devices, chunks, 2 * size, w).swapaxes(0, 1).reshape(chunks, -1, w)
+
+    def starts(s, clip):
+        return clip(s, 0, limit), clip(per_row - s - part_size + 1, 0, limit)
+
+    places = np.zeros((devices, 4, each), np.int32)
+    for at in range(devices):
+        first = 2 * each * (at // rows) + (each if at % rows >= rows // 2 else 0)
+        for i in range(each):
+            s = first + i
+            plus, minus = starts(first + i // part_size * part_size, np.clip)
+            inside = np.clip([s - plus, per_row - s - minus], 0, window - 1)
+            places[at, :, i] = [*inside, s < per_row, 1 <= s <= per_row]
+    place = lax.dynamic_index_in_dim(jnp.asarray(places), g * rows + r, 0, keepdims=False)
     first_slot = 2 * each * g + jnp.where(second, each, 0)
     first_theirs = 2 * each * g + jnp.where(second, 0, each)
-
-    give, own, places, weights = [], [], [], []
+    give, own = [], []
     for n in range(parts):
-        slots = first_slot + n * part_size + jnp.arange(part_size)
-        theirs = first_theirs + n * part_size + jnp.arange(part_size)
-        give.append(cut(jnp.where(second, start_minus(theirs), start_plus(theirs))))
-        own.append(cut(jnp.where(second, start_minus(slots), start_plus(slots))))
-        places.append(jnp.stack([slots - start_plus(slots), per_row - slots - start_minus(slots)]))
-        weights.append(jnp.stack([slots < per_row, (slots >= 1) & (slots <= per_row)]))
-    place = jnp.clip(jnp.concatenate(places, axis=1), 0, window - 1).astype(jnp.int32)
-    weight = jnp.concatenate(weights, axis=1).astype(jnp.float32)
+        plus, minus = starts(first_theirs + n * part_size, jnp.clip)
+        give.append(cut(jnp.where(second, minus, plus)))
+        plus, minus = starts(first_slot + n * part_size, jnp.clip)
+        own.append(cut(jnp.where(second, minus, plus)))
     back = exchange(
-        gops, rows, height, size, part_size // size, window, place, weight, anchors,
-        jnp.asarray(tables), features[0], jnp.stack(own), jnp.stack(give),
+        gops, rows, height, size, part_size // size, window, place, anchors,
+        jnp.asarray(tables), features[0], own, give,
         jnp.asarray(column_matrix(height, -1.0)), jnp.asarray(column_matrix(height, 1.0)),
     )
     table_back = jnp.asarray(np.ascontiguousarray(tables.reshape(-1, w).T))

time: 251 us -> 222 us (0.88)
  Pallas kernels: 230 us -> 204 us
  between operations: 5.28 us -> 0.02 us
  other arithmetic: 4.38 us -> 0 us
  local copies, waits for them, and re-layouts: 11.4 us -> 15.5 us
    pallas_call x1, Pallas kernels: 222 us -> 196 us  [exchange(): pl.pallas_call(functools.partial(exchange_kernel, frames, rows, height, c...]
    dynamic_slice x5, local copies, waits for them, and re-layouts: 8.31 us -> 13 us  [on_device(): lax.dynamic_slice_in_dim(filters, start, window, 3).reshape(-1, c)]
    another operation x1 -> x0, other arithmetic: 3.02 us -> none  [on_device(): jnp.stack(own)]
where the time goes in v4:
time: 222 us; the launch traced here: 219 us
  Pallas kernels  204 us (92%)
  local copies, waits for them, and re-layouts  15.5 us (7%)
    pallas_call x1, Pallas kernels, exchange(): pl.pallas_call(functools.partial(exchange_kernel, frames, rows, height, c...  196 us
    dynamic_slice x5, local copies, waits for them, and re-layouts, on_device(): lax.dynamic_slice_in_dim(filters, start, window, 3).reshape(-1, c)  13 us
    pallas_call x1, Pallas kernels, inverse_rows(): pl.pallas_call(functools.partial(inverse_kernel, block), grid=(h // block...  7.52 us

profile of v4, /device:TPU:31, one launch (start us, length us, event | category | flops | bytes accessed | tf_op | source)
XLA Modules:
  0.0 219.4 jit_solution(10778380027298951112)
XLA Ops:
  0.0 1.2 dynamic-slice_bitcast_fusion.place_ref
  1.2 1.3 copy.13.anchor_ref
  2.5 6.1 %constant_dynamic-slice_fusion = (bf16[3,256,2,4,128]{4,2,3,1,0:T(2,128)(2,1)S(1)}, bf16[3,256,2,4,128]{4,2,3,1,0:T(2,128)(2,1)S(1)}, bf16[3,256,2,4,128]{4,2,3,...) fusion(bf16[3,256,2,60,128]{4,2,3,1,0:T(2,128)(2,1)} %param.9, s32[]{:T(128)S(6)} %select_n.34, s32[]{:T(128)S(6)} %select_n.31, ...), kind=kLoop, calls=%fused_computation.1 | loop fusion | bytes 12582928 | tf_op jit(solution)/shard_map/dynamic_slice | solution.py:339
  8.7 1.8 copy.12
  10.4 1.7 copy.10
  12.1 1.7 copy.9
  13.8 1.7 copy.11
  15.6 196.3 %shard_map.82 = bf16[4,32,4,32,128]{4,3,2,1,0:T(8,128)(2,1)} custom-call(s32[4,8]{1,0:T(4,128)} %dynamic-slice_bitcast_fusion.place_ref, s32[4,2]{1,0:T(4,128)} %copy.13.anchor_ref, bf16[4,128,480]{2,1,0:T(8,128)(2,1)} %constant.53.clone.table_ref, bf16[32,480,128]{2,1,0:T(8,128)(2,1)} %bitcast.10, bf16[512,512]{1,0:T(8,128)(2,1)} %constant.54.clone.mf_ref, ...), custom_call_target="tpu_custom_call" | custom-call | flops 4026531840 | bytes 14155776 | tf_op jit(solution)/shard_map/pallas_call | solution.py:302
  211.9 7.5 %shard_map.83 = bf16[32,480,128]{2,1,0:T(8,128)(2,1)} custom-call(bf16[480,512]{1,0:T(8,128)(2,1)} %constant.56.clone.table_ref, bf16[512,32,128]{2,1,0:T(8,128)(2,1)} %bitcast.9, bf16[32,480,128]{2,1,0:T(8,128)(2,1)} %bitcast.11), custom_call_target="tpu_custom_call" | custom-call | flops 2013265920 | bytes 12058624 | tf_op jit(solution)/shard_map/pallas_call | solution.py:75

commit v5 on v4

--- a/solution.py
+++ b/solution.py
@@ -10,7 +10,7 @@
 from jax.experimental.pallas import tpu as pltpu
 from jax.sharding import PartitionSpec as P
 
-CHUNKS = 4
+CHUNKS = 8
 STRIDE = 13
 MESH = pl.DeviceIdType.MESH
 VMEM_LIMIT = 56 * 1024 * 1024
@@ -233,9 +233,9 @@
                 for j in range(3):
                     pieces = []
                     for p in range(2):
-                        start = (j * height + k) * lines + p * window
-                        right = p_wide[pl.ds(start + place_p, chunk, stride=lines), :]
-                        left = n_wide[pl.ds(start + place_n, chunk, stride=lines), :]
+                        start = (j * height + k) * lines + p
+                        right = p_wide[pl.ds(start + 2 * place_p, chunk, stride=lines), :]
+                        left = n_wide[pl.ds(start + 2 * place_n, chunk, stride=lines), :]
                         left = left * weight_n
                         pieces.append(right * weight_p + (left if p == 0 else -left))
                     gains.append(pieces)
@@ -336,7 +336,9 @@
     chunks = math.gcd(CHUNKS, each)
     size = each // chunks
     limit = per_row - window
-    cut = lambda start: lax.dynamic_slice_in_dim(filters, start, window, 3).reshape(-1, c)
+    cut = lambda start: (
+        lax.dynamic_slice_in_dim(filters, start, window, 3).swapaxes(2, 3).reshape(-1, c)
+    )
     tables = table.reshape(devices, chunks, 2 * size, w).swapaxes(0, 1).reshape(chunks, -1, w)
 
     def starts(s, clip):

time: 222 us -> 211 us (0.950)
  Pallas kernels: 204 us -> 198 us
  local copies, waits for them, and re-layouts: 15.5 us -> 10.6 us
    pallas_call x1, Pallas kernels: 196 us -> 190 us  [exchange(): pl.pallas_call(functools.partial(exchange_kernel, frames, rows, height, c...]
    dynamic_slice x5 -> x1, local copies, waits for them, and re-layouts: 13 us -> 8.04 us  [on_device(): lax.dynamic_slice_in_dim(filters, start, window, 3).swapaxes(2, 3)]
where the time goes in v5:
time: 211 us; the launch traced here: 209 us
  Pallas kernels  198 us (94%)
  local copies, waits for them, and re-layouts  10.6 us (5%)
    pallas_call x1, Pallas kernels, exchange(): pl.pallas_call(functools.partial(exchange_kernel, frames, rows, height, c...  190 us
    dynamic_slice x1, local copies, waits for them, and re-layouts, on_device(): lax.dynamic_slice_in_dim(filters, start, window, 3).swapaxes(2, 3)  8.04 us
    pallas_call x1, Pallas kernels, inverse_rows(): pl.pallas_call(functools.partial(inverse_kernel, block), grid=(h // block...  7.52 us

profile of v5, /device:TPU:31, one launch (start us, length us, event | category | flops | bytes accessed | tf_op | source)
XLA Modules:
  0.0 208.5 jit_solution(14125618113010144835)
XLA Ops:
  0.0 1.2 dynamic-slice_bitcast_fusion.place_ref
  1.2 1.3 copy.9.anchor_ref
  2.5 8.0 %constant_dynamic-slice_fusion = (bf16[3,256,2,4,128]{4,2,3,1,0:T(2,128)(2,1)}, bf16[3,256,2,4,128]{4,2,3,1,0:T(2,128)(2,1)}, bf16[3,256,2,4,128]{4,2,3,1,0:T(2,128)(2,1)}, bf16[3,256,2,4,128]{4,2,3,1,0:T(2,128)(2,1)}) fusion(bf16[3,256,2,60,128]{4,2,3,1,0:T(2,128)(2,1)} %param.9, s32[]{:T(128)S(6)} %select_n.34, s32[]{:T(128)S(6)} %select_n.31, ...), kind=kLoop, calls=%fused_computation.1 | loop fusion | bytes 12582928 | tf_op jit(solution)/shard_map/dynamic_slice | solution.py:340
  10.6 190.4 %shard_map.82 = bf16[8,32,2,32,128]{4,3,2,1,0:T(8,128)(2,1)} custom-call(s32[4,8]{1,0:T(4,128)} %dynamic-slice_bitcast_fusion.place_ref, s32[4,2]{1,0:T(4,128)} %copy.9.anchor_ref, bf16[8,64,480]{2,1,0:T(8,128)(2,1)} %constant.53.clone.table_ref, bf16[32,480,128]{2,1,0:T(8,128)(2,1)} %bitcast.18, bf16[512,512]{1,0:T(8,128)(2,1)} %constant.54.clone.mf_ref, ...), custom_call_target="tpu_custom_call" | custom-call | flops 4026531840 | bytes 14155776 | tf_op jit(solution)/shard_map/pallas_call | solution.py:302
  201.0 7.5 %shard_map.83 = bf16[32,480,128]{2,1,0:T(8,128)(2,1)} custom-call(bf16[480,512]{1,0:T(8,128)(2,1)} %constant.56.clone.table_ref, bf16[512,32,128]{2,1,0:T(8,128)(2,1)} %bitcast.17, bf16[32,480,128]{2,1,0:T(8,128)(2,1)} %bitcast.19), custom_call_target="tpu_custom_call" | custom-call | flops 2013265920 | bytes 12058624 | tf_op jit(solution)/shard_map/pallas_call | solution.py:75
